TPU v7x, 512 devices: a whole 4x4x16 slice. The times are simulated.
512 devices in a mesh: frame: 64 (over z, y_lo, core), head: 8 (over x, y_hi).
Axes of the slice: x: 4, y: 4 (y_hi: 2, y_lo: 2; y = y_hi * 2 + y_lo), z: 16, core: 2. Of those that a mesh axis runs over, the one named last changes fastest.
Arguments:
- queries: bfloat16 [64, 512, 5120], P('frame', 'head'), may hold values from -80 to 80
- keys: bfloat16 [64, 512, 5120], P('frame', 'head'), may hold values from -80 to 80
- values: bfloat16 [64, 512, 5120], P('frame', 'head'), may hold values from -6 to 6
- residual: bfloat16 [64, 512, 5120], P('frame', 'head'), may hold values from -4 to 4
- q_gain: float32 [5120], replicated, may hold values from 1 to 3
- k_gain: float32 [5120], replicated, may hold values from 1 to 3
- gate_table: float32 [128, 5120], P(None, 'head'), may hold values from 0.5 to 3
- levels: int32 [64], P('frame'), may hold values from 0 to 127, as said below
- offsets: int32 [64], P('frame'), may hold values from 0 to 2, as said below
- incoming: bfloat16 [512, 5120], P('head'), may hold values from -6 to 6
Outputs:
- queue_next: bfloat16 [64, 512, 5120], P('frame', 'head')
Inputs may be any that keep to these rules, and one draw needn't show every extreme that they name: levels rise strictly along the queue; levels[f] is 2 f or 2 f + 1, with levels[0] = 0 and the last frame at 127. offsets[f] = (f + s) mod 3 for one shift s of 0 to 2: the windows are runs of 3 consecutive frames starting at frame -s.
All inputs are finite; a program needn't handle non-finite values.
Results may differ from a plain program's by a relative error of at most 0.0098.
Values may be sent and summed in bfloat16 or wider, within the bound.
No kernel may reach another device: no remote copies, remote signals or barrier semaphores. Data moves between devices by JAX's collectives and lax.ppermute only.
A program may use at most 64 MiB of HBM per device.

v0:
```python
import functools
import math
import jax
import jax.numpy as jnp
from jax import lax
from jax.experimental import pallas as pl
from jax.experimental.pallas import tpu as pltpu
from jax.sharding import Mesh, PartitionSpec as P

HD = 128
W = 3
REACH = W - 1
SLOTS = 4
GROUPS = 8
OWN = 5
ROWS = 64
PART = ROWS // SLOTS
KV_ROWS = 2 * (ROWS + PART)
Q_ROWS = 2 * ROWS + 16
O_ROWS = 2 * ROWS + 16
LOG2E = math.log2(math.e)
SCALE = LOG2E / math.sqrt(HD)
FAR = 1e30
VMEM = pltpu.VMEM


def params():
    return pltpu.CompilerParams(vmem_limit_bytes=48 * 1024 * 1024)


def lanes(head):
    return slice(head * HD, (head + 1) * HD)


def scale_of(wide):
    return lax.rsqrt(jnp.mean(wide * wide, axis=-1, keepdims=True) + 1e-06)


def pack_kv_kernel(keys, values, gain, out):
    by = scale_of(keys[...].astype(jnp.float32))
    for group in range(GROUPS):
        for own in range(OWN):
            at = lanes(group * OWN + own)
            key = (keys[:, at].astype(jnp.float32) * by * gain[:, at]).astype(jnp.bfloat16)
            value = values[:, at]
            if own < SLOTS:
                out[own * GROUPS + group, 0:ROWS, :] = key
                out[own * GROUPS + group, ROWS + PART : 2 * ROWS + PART, :] = value
            else:
                for slot in range(SLOTS):
                    part = slice(slot * PART, (slot + 1) * PART)
                    out[slot * GROUPS + group, ROWS : ROWS + PART, :] = key[part]
                    out[slot * GROUPS + group, 2 * ROWS + PART : KV_ROWS, :] = value[part]


def pack_q_kernel(levels, queries, gain, out):
    by = scale_of(queries[...].astype(jnp.float32))
    level = jnp.full((16, HD), levels[0], jnp.int32).astype(jnp.float32).astype(jnp.bfloat16)
    for group in range(GROUPS):
        for own in range(OWN):
            at = lanes(group * OWN + own)
            query = (queries[:, at].astype(jnp.float32) * by * gain[:, at]).astype(jnp.bfloat16)
            if own < SLOTS:
                out[own * GROUPS + group, 0:ROWS, :] = query
                out[own * GROUPS + group, 2 * ROWS : Q_ROWS, :] = level
            else:
                for slot in range(SLOTS):
                    out[slot * GROUPS + group, ROWS : 2 * ROWS, :] = query


def attend_kernel(
    frames, first_out, planes, tile, offsets, left, mine, right, queries, gates, out, key_all, value_all, key_part, value_part
):
    plane = lax.axis_index("plane")
    slot = lax.axis_index("slot")
    count = planes * SLOTS
    phase = lax.rem(offsets[0] + W * count - (plane * SLOTS + slot), W)
    blocks = 2 * REACH + SLOTS
    ones = jnp.ones((ROWS * GROUPS, HD), jnp.bfloat16)
    for j in range(min(frames), max(frames) + 2 * REACH + 1):
        if j < REACH:
            ref, base = left, j * GROUPS
        elif j < REACH + SLOTS:
            ref, base = mine, (j - REACH) * GROUPS
        else:
            ref, base = right, (j - REACH - SLOTS) * GROUPS
        from_all = slice(base, base + GROUPS)
        key_all[j] = ref[from_all, 0:ROWS, :].reshape(ROWS * GROUPS, HD)
        key_part[j] = ref[from_all, ROWS : ROWS + PART, :].reshape(PART * GROUPS, HD)
        value_all[j, :, 0:HD] = ref[from_all, ROWS + PART : 2 * ROWS + PART, :].reshape(ROWS * GROUPS, HD)
        value_all[j, :, HD:] = ones
        value_part[j, :, 0:HD] = ref[from_all, 2 * ROWS + PART : KV_ROWS, :].reshape(PART * GROUPS, HD)
        value_part[j, :, HD:] = ones[: PART * GROUPS]

    def softmaxed(query, key_ref, value_ref, start, allowed):
        scores = [
            lax.dot_general(
                query, key_ref[start + b], (((1,), (1,)), ((), ())), preferred_element_type=jnp.float32
            )
            for b in range(W)
        ]
        tops = [
            jnp.where(allowed[b], jnp.max(scores[b], axis=-1, keepdims=True), -FAR) for b in range(W)
        ]
        top = functools.reduce(jnp.maximum, tops)
        total = None
        for b in range(W):
            weights = jnp.exp2((scores[b] - jnp.where(allowed[b], top, FAR)) * SCALE)
            term = jnp.dot(
                weights.astype(jnp.bfloat16), value_ref[start + b], preferred_element_type=jnp.float32
            )
            total = term if total is None else total + term
        return top, total[:, :HD], total[:, HD:]

    row = lax.broadcasted_iota(jnp.int32, (16, HD), 0)
    level_row = lax.broadcasted_iota(jnp.int32, (gates.shape[0], HD), 0).astype(jnp.float32)
    spot = lax.broadcasted_iota(jnp.int32, (ROWS * GROUPS, HD), 0) % ROWS == lax.broadcasted_iota(
        jnp.int32, (ROWS * GROUPS, HD), 1
    )
    blocks_of = tile // ROWS
    for i in frames:
        frame = plane * SLOTS + i
        offset = lax.rem(frame + phase, W)
        start = i + REACH - offset
        allowed = [
            (frame - offset + b >= 0) & (frame - offset + b < count) for b in range(W)
        ]
        level = queries[i * GROUPS, 2 * ROWS : 2 * ROWS + 1, :].astype(jnp.float32)
        picked = level_row == level

        def gate_of(at):
            return jnp.sum(jnp.where(picked, gates[:, at], 0.0), axis=0, keepdims=True)

        gate = gate_of(pl.ds(pl.multiple_of(slot * HD, HD), HD))
        gate_shared = gate_of(pl.ds(SLOTS * HD, HD))
        to = (i - frames[0] + first_out) * GROUPS

        def step(n, carry):
            query = queries[pl.ds(i * GROUPS + n * blocks_of, blocks_of), 0:ROWS, :].reshape(tile, HD)
            _, numer, total = softmaxed(query, key_all, value_all, start, allowed)
            done = (numer / total * gate).astype(jnp.bfloat16).reshape(blocks_of, ROWS, HD)
            out[pl.ds(to + n * blocks_of, blocks_of), 0:ROWS, :] = done
            return carry

        lax.fori_loop(0, ROWS * GROUPS // tile, step, 0)

        query = queries[i * GROUPS : (i + 1) * GROUPS, ROWS : 2 * ROWS, :].reshape(ROWS * GROUPS, HD)
        top, numer, total = softmaxed(query, key_part, value_part, start, allowed)
        done = (numer / total * gate_shared).astype(jnp.bfloat16).reshape(GROUPS, ROWS, HD)
        out[to : to + GROUPS, ROWS : 2 * ROWS, :] = done
        weight = top * SCALE + jnp.log(total) * LOG2E
        weight = jnp.where(spot, weight, 0.0).reshape(GROUPS, ROWS, HD).sum(axis=1)
        high = weight.astype(jnp.bfloat16).astype(jnp.float32)
        rest = weight - high
        middle = rest.astype(jnp.bfloat16).astype(jnp.float32)
        low = rest - middle
        for t in range(GROUPS):
            at = slice(t, t + 1)
            three = jnp.where(row == 0, high[at], jnp.where(row == 1, middle[at], low[at]))
            out[to + t, 2 * ROWS : O_ROWS, :] = three.astype(jnp.bfloat16)


def combine_kernel(parts, residual, incoming, out):
    first = (lax.axis_index("plane") == 0) & (lax.axis_index("slot") == 0)

    @pl.when(first)
    def _():
        out[...] = incoming[...]

    @pl.when(jnp.logical_not(first))
    def _():
        sent = parts[:, 2 * ROWS : O_ROWS, :].astype(jnp.float32)
        row = lax.broadcasted_iota(jnp.int32, sent.shape, 1)
        weight = jnp.sum(jnp.where(row < 3, sent, 0.0), axis=1).reshape(SLOTS, GROUPS, HD)
        weight = jnp.exp2(weight - jnp.max(weight, axis=0, keepdims=True))
        weight = weight / jnp.sum(weight, axis=0, keepdims=True)
        weight = weight.reshape(SLOTS * GROUPS, HD)
        weight = jnp.concatenate([weight, jnp.zeros((HD - SLOTS * GROUPS, HD), jnp.float32)])
        weight = weight.T[:ROWS]
        for group in range(GROUPS):
            shared = None
            for slot in range(SLOTS):
                r = slot * GROUPS + group
                at = lanes(group * OWN + slot)
                updated = residual[:, at].astype(jnp.float32) + parts[r, 0:ROWS, :].astype(jnp.float32)
                out[:, at] = updated.astype(jnp.bfloat16)
                term = weight[:, r : r + 1] * parts[r, ROWS : 2 * ROWS, :].astype(jnp.float32)
                shared = term if shared is None else shared + term
            at = lanes(group * OWN + SLOTS)
            shared = shared.astype(jnp.bfloat16).astype(jnp.float32)
            out[:, at] = (residual[:, at].astype(jnp.float32) + shared).astype(jnp.bfloat16)


def whole(count):
    return [pl.BlockSpec(memory_space=VMEM)] * count


def on_device(
    planes, queries, keys, values, residual, q_gain, k_gain, gate_table, levels, offsets, incoming
):
    smem = pl.BlockSpec(memory_space=pltpu.SMEM)
    dests = SLOTS * GROUPS
    exchange = lambda x: lax.all_to_all(x, ("slot", "group"), 0, 0, tiled=True)
    up = [(z, (z + 1) % planes) for z in range(planes)]
    down = [(z, (z - 1) % planes) for z in range(planes)]
    count = planes * SLOTS

    kv = pl.pallas_call(
        pack_kv_kernel,
        out_shape=jax.ShapeDtypeStruct((dests, KV_ROWS, HD), jnp.bfloat16),
        in_specs=whole(3),
        out_specs=whole(1)[0],
        compiler_params=params(),
        name="pack_kv",
    )(keys[0], values[0], k_gain[None])
    kv = exchange(kv)
    packed = pl.pallas_call(
        pack_q_kernel,
        out_shape=jax.ShapeDtypeStruct((dests, Q_ROWS, HD), jnp.bfloat16),
        in_specs=[smem] + whole(2),
        out_specs=whole(1)[0],
        compiler_params=params(),
        name="pack_q",
    )(levels, queries[0], q_gain[None])
    query = exchange(packed)
    edge = REACH * GROUPS
    right = lax.ppermute(kv[:edge], "plane", down)
    left = lax.ppermute(kv[dests - edge :], "plane", up)
    moved = lax.ppermute(residual[0], ("plane", "slot"), [(f, (f + 1) % count) for f in range(count)])

    def attend(frames, first_out, slots_out, name):
        blocks = 2 * REACH + SLOTS
        units = len(frames)
        return pl.pallas_call(
            functools.partial(attend_kernel, frames, first_out, planes, 256),
            out_shape=jax.ShapeDtypeStruct((slots_out * GROUPS, O_ROWS, HD), jnp.bfloat16),
            in_specs=[smem] + whole(5),
            out_specs=whole(1)[0],
            scratch_shapes=[
                VMEM((blocks, ROWS * GROUPS, HD), jnp.bfloat16),
                VMEM((blocks, ROWS * GROUPS, 2 * HD), jnp.bfloat16),
                VMEM((blocks, PART * GROUPS, HD), jnp.bfloat16),
                VMEM((blocks, PART * GROUPS, 2 * HD), jnp.bfloat16),
            ],
            compiler_params=params(),
            cost_estimate=pl.CostEstimate(
                flops=units * 500_000_000, bytes_accessed=4_000_000, transcendentals=units * 1_000_000
            ),
            name=name,
        )(offsets, left, kv, right, query, gate_table)

    last = lax.ppermute(attend((SLOTS - 1,), 0, 1, "attend_last"), "plane", up)
    others = attend(tuple(range(SLOTS - 1)), 1, SLOTS, "attend_others")
    parts = exchange(lax.dynamic_update_slice(others, last, (0, 0, 0)))
    updated = pl.pallas_call(
        combine_kernel,
        out_shape=jax.ShapeDtypeStruct(incoming.shape, jnp.bfloat16),
        in_specs=whole(3),
        out_specs=whole(1)[0],
        compiler_params=params(),
        name="combine",
    )(parts, moved, incoming)
    return updated[None]


def solution(mesh):
    planes = mesh.shape["frame"] // SLOTS
    inner = Mesh(
        mesh.devices.reshape(planes, SLOTS, GROUPS), ("plane", "slot", "group")
    )
    frame = ("plane", "slot")
    tokens = P(frame, "group", None)
    placed = (
        tokens,
        tokens,
        tokens,
        tokens,
        P(),
        P(),
        P(None, "group"),
        P(frame),
        P(frame),
        P("group", None),
    )
    return jax.shard_map(
        functools.partial(on_device, planes), mesh=inner, in_specs=placed, out_specs=tokens, check_vma=False
    )
```

profile of v0, /device:TPU:1, one launch (start us, length us, event | category | flops | bytes accessed | tf_op | source)
XLA Modules:
  0.0 117.1 jit_solution(14678114895171638788)
XLA Ops:
  0.0 1.1 copy-done.1
  1.1 1.1 copy-done.2
  2.2 0.7 copy-done.6
  2.9 1.4 %pack_kv.1 = bf16[32,160,128]{2,1,0:T(8,128)(2,1)} custom-call(bf16[64,5120]{1,0:T(8,128)(2,1)S(1)} %bitcast.7, bf16[64,5120]{1,0:T(8,128)(2,1)S(1)} %bitcast.8, f32[1,5120]{1,0:T(1,128)S(1)} %bitcast.10), custom_call_target="tpu_custom_call" | custom-call | tf_op jit(solution)/shard_map/pack_kv/pallas_call | solution.py:208
  4.3 10.7 %all-to-all-start = ((bf16[32,160,128]{2,1,0:T(8,128)(2,1)}), bf16[32,160,128]{2,1,0:T(8,128)(2,1)S(1)}, u32[]{:S(2)}, u32[]{:S(2)}) async-start(bf16[32,160,128]{2,1,0:T(8,128)(2,1)} %pack_kv.1), calls=%async_computation | async-start | bytes 2621440 | tf_op jit(solution)/shard_map/all_to_all | solution.py:203
  15.6 0.0 copy-done.3
  15.6 0.0 copy-done.7
  15.7 0.3 pack_q.1
  16.0 0.0 copy-start
  16.0 1.0 copy-done
  17.0 18.4 %all-to-all-done.mine = bf16[32,160,128]{2,1,0:T(8,128)(2,1)S(1)} async-done(((bf16[32,160,128]{2,1,0:T(8,128)(2,1)}), bf16[32,160,128]{2,1,0:T(8,128)(2,1)S(1)}, u32[]{:S(2)}, u32[]{:S(2)}) %all-to-all-start) | async-done | bytes 1310752 | tf_op jit(solution)/shard_map/all_to_all | solution.py:203
  35.4 4.0 %all-to-all-start.1 = ((bf16[32,144,128]{2,1,0:T(8,128)(2,1)}), bf16[32,144,128]{2,1,0:T(8,128)(2,1)S(1)}, u32[]{:S(2)}, u32[]{:S(2)}) async-start(bf16[32,144,128]{2,1,0:T(8,128)(2,1)} %copy-done), calls=%async_computation.1 | async-start | bytes 2359296 | tf_op jit(solution)/shard_map/all_to_all | solution.py:203
  39.4 0.0 copy-start.5
  39.4 1.1 fusion
  40.6 1.9 %collective-permute-start = (bf16[16,160,128]{2,1,0:T(8,128)(2,1)}, bf16[16,160,128]{2,1,0:T(8,128)(2,1)S(1)}, u32[]{:S(2)}, u32[]{:S(2)}) collective-permute-start(bf16[16,160,128]{2,1,0:T(8,128)(2,1)} %get-tuple-element.6), channel_id=1, source_target_pairs={{0,32},{32,64},{64,96},{96,128},{128,160},{160,192},{192,224},{224... | collective-permute-start | bytes 1966088 | tf_op jit(solution)/shard_map/ppermute | solution.py:228
  42.5 9.2 %collective-permute-start.1 = (bf16[16,160,128]{2,1,0:T(8,128)(2,1)}, bf16[16,160,128]{2,1,0:T(8,128)(2,1)}, u32[]{:S(2)}, u32[]{:S(2)}) collective-permute-start(bf16[16,160,128]{2,1,0:T(8,128)(2,1)} %get-tuple-element.5), channel_id=1, source_target_pairs={{0,480},{32,0},{64,32},{96,64},{128,96},{160,128},{192,160},{224,1... | collective-permute-start | bytes 1966088 | tf_op jit(solution)/shard_map/ppermute | solution.py:227
  52.4 6.1 %all-to-all-done.1.queries = bf16[32,144,128]{2,1,0:T(8,128)(2,1)S(1)} async-done(((bf16[32,144,128]{2,1,0:T(8,128)(2,1)}), bf16[32,144,128]{2,1,0:T(8,128)(2,1)S(1)}, u32[]{:S(2)}, u32[]{:S(2)}) %all-to-all-start.1) | async-done | bytes 1179680 | tf_op jit(solution)/shard_map/all_to_all | solution.py:203
  58.4 6.5 %collective-permute-done.left = bf16[16,160,128]{2,1,0:T(8,128)(2,1)S(1)} collective-permute-done((bf16[16,160,128]{2,1,0:T(8,128)(2,1)}, bf16[16,160,128]{2,1,0:T(8,128)(2,1)S(1)}, u32[]{:S(2)}, u32[]{:S(2)}) %collective-permute-start) | collective-permute-done | bytes 655392 | tf_op jit(solution)/shard_map/ppermute | solution.py:228
  64.9 1.0 collective-permute-done.1.right
  65.9 0.0 copy-done.5
  65.9 4.7 %attend_last.1 = bf16[8,144,128]{2,1,0:T(8,128)(2,1)S(1)} custom-call(s32[1]{0:T(128)S(6)} %copy.13.offsets, bf16[16,160,128]{2,1,0:T(8,128)(2,1)S(1)} %collective-permute-done.left, bf16[32,160,128]{2,1,0:T(8,128)(2,1)S(1)} %all-to-all-done.mine, bf16[16,160,128]{2,1,0:T(8,128)(2,1)} %collective-permute-done.1.right, ...), custom_call_target="tpu_custom_call" | custom-call | flops 500000000 | bytes 4000000 | tf_op jit(solution)/shard_map/attend_last/pallas_call | solution.py:234
  70.6 1.9 %collective-permute-start.2 = (bf16[8,144,128]{2,1,0:T(8,128)(2,1)S(1)}, bf16[8,144,128]{2,1,0:T(8,128)(2,1)S(1)}, u32[]{:S(2)}, u32[]{:S(2)}) collective-permute-start(bf16[8,144,128]{2,1,0:T(8,128)(2,1)S(1)} %attend_last.1), channel_id=1, source_target_pairs={{0,32},{32,64},{64,96},{96,128},{128,160},{160,192},{192,224},{224... | collective-permute-start | bytes 884744 | tf_op jit(solution)/shard_map/ppermute | solution.py:252
  72.5 12.5 %attend_others.1 = bf16[32,144,128]{2,1,0:T(8,128)(2,1)} custom-call(s32[1]{0:T(128)S(6)} %copy.13.offsets, bf16[16,160,128]{2,1,0:T(8,128)(2,1)S(1)} %collective-permute-done.left, bf16[32,160,128]{2,1,0:T(8,128)(2,1)S(1)} %all-to-all-done.mine, bf16[16,160,128]{2,1,0:T(8,128)(2,1)} %collective-permute-done.1.right, ...), custom_call_target="tpu_custom_call" | custom-call | flops 1500000000 | bytes 4000000 | tf_op jit(solution)/shard_map/attend_others/pallas_call | solution.py:234
  85.0 0.0 collective-permute-done.2
  85.0 0.7 constant_dynamic-update-slice_fusion
  85.7 8.2 %all-to-all-start.2 = ((bf16[32,144,128]{2,1,0:T(8,128)(2,1)}), bf16[32,144,128]{2,1,0:T(8,128)(2,1)S(1)}, u32[]{:S(2)}, u32[]{:S(2)}) async-start(bf16[32,144,128]{2,1,0:T(8,128)(2,1)} %constant_dynamic-update-slice_fusion), calls=%async_computation.2 | async-start | bytes 2359296 | tf_op jit(solution)/shard_map/all_to_all | solution.py:203
  93.9 0.0 copy-done.8
  93.9 3.5 %collective-permute-start.3 = (bf16[64,5120]{1,0:T(8,128)(2,1)S(1)}, bf16[64,5120]{1,0:T(8,128)(2,1)S(1)}, u32[]{:S(2)}, u32[]{:S(2)}) collective-permute-start(bf16[64,5120]{1,0:T(8,128)(2,1)S(1)} %bitcast.12), channel_id=1, source_target_pairs={{0,8},{8,16},{16,24},{24,32},{32,40},{40,48},{48,56},{56,64},{64,7... | collective-permute-start | bytes 1966088 | tf_op jit(solution)/shard_map/ppermute | solution.py:229
  97.5 16.7 %collective-permute-done.3.residual = bf16[64,5120]{1,0:T(8,128)(2,1)S(1)} collective-permute-done((bf16[64,5120]{1,0:T(8,128)(2,1)S(1)}, bf16[64,5120]{1,0:T(8,128)(2,1)S(1)}, u32[]{:S(2)}, u32[]{:S(2)}) %collective-permute-start.3) | collective-permute-done | bytes 655392 | tf_op jit(solution)/shard_map/ppermute | solution.py:229
  114.2 1.4 %all-to-all-done.2.parts = bf16[32,144,128]{2,1,0:T(8,128)(2,1)S(1)} async-done(((bf16[32,144,128]{2,1,0:T(8,128)(2,1)}), bf16[32,144,128]{2,1,0:T(8,128)(2,1)S(1)}, u32[]{:S(2)}, u32[]{:S(2)}) %all-to-all-start.2) | async-done | bytes 1179680 | tf_op jit(solution)/shard_map/all_to_all | solution.py:203
  115.6 0.0 copy-done.4
  115.6 1.5 %combine.1 = bf16[64,5120]{1,0:T(8,128)(2,1)} custom-call(bf16[32,144,128]{2,1,0:T(8,128)(2,1)S(1)} %all-to-all-done.2.parts, bf16[64,5120]{1,0:T(8,128)(2,1)S(1)} %collective-permute-done.3.residual, bf16[64,5120]{1,0:T(8,128)(2,1)S(1)} %copy-done.4), custom_call_target="tpu_custom_call" | custom-call | tf_op jit(solution)/shard_map/combine/pallas_call | solution.py:255
  (7 shorter events, 0.0 us)
Async XLA Ops:
  0.0 1.1 copy-start.1
  1.1 1.1 copy-start.2
  2.2 0.7 copy-start.6
  4.3 11.3 %copy-start.3 = (bf16[1,64,5120]{2,1,0:T(8,128)(2,1)S(1)}, bf16[1,64,5120]{2,1,0:T(8,128)(2,1)}, u32[]{:S(2)}) copy-start(bf16[1,64,5120]{2,1,0:T(8,128)(2,1)} %param.10) | copy-start | bytes 1966084
  4.3 11.3 %copy-start.7 = (f32[5120]{0:T(1024)S(1)}, f32[5120]{0:T(1024)}, u32[]{:S(2)}) copy-start(f32[5120]{0:T(1024)} %param.14) | copy-start | bytes 61444
  4.3 31.1 %all-to-all-start = ((bf16[32,160,128]{2,1,0:T(8,128)(2,1)}), bf16[32,160,128]{2,1,0:T(8,128)(2,1)S(1)}, u32[]{:S(2)}, u32[]{:S(2)}) async-start(bf16[32,160,128]{2,1,0:T(8,128)(2,1)} %pack_kv.1), calls=%async_computation | async-start | bytes 2621440 | tf_op jit(solution)/shard_map/all_to_all | solution.py:203
  16.0 1.1 copy-start
  35.4 23.0 %all-to-all-start.1 = ((bf16[32,144,128]{2,1,0:T(8,128)(2,1)}), bf16[32,144,128]{2,1,0:T(8,128)(2,1)S(1)}, u32[]{:S(2)}, u32[]{:S(2)}) async-start(bf16[32,144,128]{2,1,0:T(8,128)(2,1)} %copy-done), calls=%async_computation.1 | async-start | bytes 2359296 | tf_op jit(solution)/shard_map/all_to_all | solution.py:203
  39.4 26.5 %copy-start.5 = (f32[128,640]{1,0:T(8,128)S(1)}, f32[128,640]{1,0:T(8,128)}, u32[]{:S(2)}) copy-start(f32[128,640]{1,0:T(8,128)} %gates.3) | copy-start | bytes 983044
  40.6 24.4 %collective-permute-start = (bf16[16,160,128]{2,1,0:T(8,128)(2,1)}, bf16[16,160,128]{2,1,0:T(8,128)(2,1)S(1)}, u32[]{:S(2)}, u32[]{:S(2)}) collective-permute-start(bf16[16,160,128]{2,1,0:T(8,128)(2,1)} %get-tuple-element.6), channel_id=1, source_target_pairs={{0,32},{32,64},{64,96},{96,128},{128,160},{160,192},{192,224},{224... | collective-permute-start | bytes 1966088 | tf_op jit(solution)/shard_map/ppermute | solution.py:228
  42.5 23.4 %collective-permute-start.1 = (bf16[16,160,128]{2,1,0:T(8,128)(2,1)}, bf16[16,160,128]{2,1,0:T(8,128)(2,1)}, u32[]{:S(2)}, u32[]{:S(2)}) collective-permute-start(bf16[16,160,128]{2,1,0:T(8,128)(2,1)} %get-tuple-element.5), channel_id=1, source_target_pairs={{0,480},{32,0},{64,32},{96,64},{128,96},{160,128},{192,160},{224,1... | collective-permute-start | bytes 1966088 | tf_op jit(solution)/shard_map/ppermute | solution.py:227
  70.6 14.4 %collective-permute-start.2 = (bf16[8,144,128]{2,1,0:T(8,128)(2,1)S(1)}, bf16[8,144,128]{2,1,0:T(8,128)(2,1)S(1)}, u32[]{:S(2)}, u32[]{:S(2)}) collective-permute-start(bf16[8,144,128]{2,1,0:T(8,128)(2,1)S(1)} %attend_last.1), channel_id=1, source_target_pairs={{0,32},{32,64},{64,96},{96,128},{128,160},{160,192},{192,224},{224... | collective-permute-start | bytes 884744 | tf_op jit(solution)/shard_map/ppermute | solution.py:252
  85.7 8.2 %copy-start.8 = (bf16[1,64,5120]{2,1,0:T(8,128)(2,1)S(1)}, bf16[1,64,5120]{2,1,0:T(8,128)(2,1)}, u32[]{:S(2)}) copy-start(bf16[1,64,5120]{2,1,0:T(8,128)(2,1)} %param.13) | copy-start | bytes 1966084
  85.7 29.8 %copy-start.4 = (bf16[64,5120]{1,0:T(8,128)(2,1)S(1)}, bf16[64,5120]{1,0:T(8,128)(2,1)}, u32[]{:S(2)}) copy-start(bf16[64,5120]{1,0:T(8,128)(2,1)} %incoming.1) | copy-start | bytes 1966084
  85.7 29.8 %all-to-all-start.2 = ((bf16[32,144,128]{2,1,0:T(8,128)(2,1)}), bf16[32,144,128]{2,1,0:T(8,128)(2,1)S(1)}, u32[]{:S(2)}, u32[]{:S(2)}) async-start(bf16[32,144,128]{2,1,0:T(8,128)(2,1)} %constant_dynamic-update-slice_fusion), calls=%async_computation.2 | async-start | bytes 2359296 | tf_op jit(solution)/shard_map/all_to_all | solution.py:203
  93.9 20.3 %collective-permute-start.3 = (bf16[64,5120]{1,0:T(8,128)(2,1)S(1)}, bf16[64,5120]{1,0:T(8,128)(2,1)S(1)}, u32[]{:S(2)}, u32[]{:S(2)}) collective-permute-start(bf16[64,5120]{1,0:T(8,128)(2,1)S(1)} %bitcast.12), channel_id=1, source_target_pairs={{0,8},{8,16},{16,24},{24,32},{32,40},{40,48},{48,56},{56,64},{64,7... | collective-permute-start | bytes 1966088 | tf_op jit(solution)/shard_map/ppermute | solution.py:229
where the time goes:
time: 118 us; the launch traced here: 117 us
  waiting for transfers between devices  50 us (42%)
  starting transfers between devices  39.4 us (33%)
  Pallas kernels  20.4 us (17%)
  local copies, waits for them, and re-layouts  5.84 us (5%)
  between operations  1.41 us (1%)
    all_to_all x3, waiting for transfers between devices, on_device(): exchange = lambda x: lax.all_to_all(x, ('slot', 'group'), 0, 0, tiled=True)  25.8 us
    all_to_all x3, starting transfers between devices, on_device(): exchange = lambda x: lax.all_to_all(x, ('slot', 'group'), 0, 0, tiled=True)  22.8 us
    pallas_call x2, Pallas kernels, attend(): pl.pallas_call(functools.partial(attend_kernel, frames, first_out, planes...  17.2 us
    ppermute x1, waiting for transfers between devices, on_device(): lax.ppermute(residual[0], ('plane', 'slot'), [(f, (f + 1) % count) for f...  16.7 us
    ppermute x1, starting transfers between devices, on_device(): right = lax.ppermute(kv[:edge], 'plane', down)  9.24 us
    ppermute x1, waiting for transfers between devices, on_device(): left = lax.ppermute(kv[dests - edge:], 'plane', up)  6.52 us
    unnamed x18, local copies, waits for them, and re-layouts  3.97 us
    ppermute x1, starting transfers between devices, on_device(): lax.ppermute(residual[0], ('plane', 'slot'), [(f, (f + 1) % count) for f...  3.54 us
  transfers between devices with their start and end apart: 7, of which 6 were waited for; matrix products, arithmetic and copies ran while one was open for 1% of the time, Pallas kernels for 11%

commit v1 on v0

--- a/solution.py
+++ b/solution.py
@@ -15,17 +15,18 @@
 OWN = 5
 ROWS = 64
 PART = ROWS // SLOTS
+CHUNK = 16
 KV_ROWS = 2 * (ROWS + PART)
 Q_ROWS = 2 * ROWS + 16
 O_ROWS = 2 * ROWS + 16
-LOG2E = math.log2(math.e)
-SCALE = LOG2E / math.sqrt(HD)
+SCALE = 1.0 / math.sqrt(HD)
 FAR = 1e30
 VMEM = pltpu.VMEM
-
-
-def params():
-    return pltpu.CompilerParams(vmem_limit_bytes=48 * 1024 * 1024)
+HBM = pl.BlockSpec(memory_space=pltpu.HBM)
+
+
+def params(mib=48):
+    return pltpu.CompilerParams(vmem_limit_bytes=mib * 1024 * 1024)
 
 
 def lanes(head):
@@ -36,21 +37,46 @@
     return lax.rsqrt(jnp.mean(wide * wide, axis=-1, keepdims=True) + 1e-06)
 
 
-def pack_kv_kernel(keys, values, gain, out):
-    by = scale_of(keys[...].astype(jnp.float32))
+def pack_kv_kernel(keys_in, values_in, gain, out, keys, values, blocks, in_sems, out_sems):
+    chunks = ROWS // CHUNK
+    reads = []
+    for n, (source, target) in enumerate(((keys_in, keys), (values_in, values))):
+        for c in range(chunks):
+            at = pl.ds(c * CHUNK, CHUNK)
+            read = pltpu.make_async_copy(source.at[at], target.at[at], in_sems.at[n * chunks + c])
+            read.start()
+            reads.append(read)
+    scales = []
+    for c in range(chunks):
+        reads[c].wait()
+        scales.append(scale_of(keys[c * CHUNK : (c + 1) * CHUNK, :].astype(jnp.float32)))
+    by = jnp.concatenate(scales)
+    for read in reads[chunks:]:
+        read.wait()
+
+    def pair(head):
+        at = lanes(head)
+        key = (keys[:, at].astype(jnp.float32) * by * gain[:, at]).astype(jnp.bfloat16)
+        return key, values[:, at]
+
     for group in range(GROUPS):
-        for own in range(OWN):
-            at = lanes(group * OWN + own)
-            key = (keys[:, at].astype(jnp.float32) * by * gain[:, at]).astype(jnp.bfloat16)
-            value = values[:, at]
-            if own < SLOTS:
-                out[own * GROUPS + group, 0:ROWS, :] = key
-                out[own * GROUPS + group, ROWS + PART : 2 * ROWS + PART, :] = value
-            else:
-                for slot in range(SLOTS):
-                    part = slice(slot * PART, (slot + 1) * PART)
-                    out[slot * GROUPS + group, ROWS : ROWS + PART, :] = key[part]
-                    out[slot * GROUPS + group, 2 * ROWS + PART : KV_ROWS, :] = value[part]
+        key, value = pair(group * OWN + SLOTS)
+        for slot in range(SLOTS):
+            part = slice(slot * PART, (slot + 1) * PART)
+            blocks[slot * GROUPS + group, ROWS : ROWS + PART, :] = key[part]
+            blocks[slot * GROUPS + group, 2 * ROWS + PART : KV_ROWS, :] = value[part]
+    writes = []
+    for slot in range(SLOTS):
+        for group in range(GROUPS):
+            key, value = pair(group * OWN + slot)
+            blocks[slot * GROUPS + group, 0:ROWS, :] = key
+            blocks[slot * GROUPS + group, ROWS + PART : 2 * ROWS + PART, :] = value
+        at = pl.ds(slot * GROUPS, GROUPS)
+        write = pltpu.make_async_copy(blocks.at[at], out.at[at], out_sems.at[slot])
+        write.start()
+        writes.append(write)
+    for write in writes:
+        write.wait()
 
 
 def pack_q_kernel(levels, queries, gain, out):
@@ -69,7 +95,7 @@
 
 
 def attend_kernel(
-    frames, first_out, planes, tile, offsets, left, mine, right, queries, gates, out, key_all, value_all, key_part, value_part
+    frames, first_out, planes, tile, offsets, left, mine, right, queries, gates, out_ref, key_all, value_all, key_part, value_part, out, sems
 ):
     plane = lax.axis_index("plane")
     slot = lax.axis_index("slot")
@@ -100,12 +126,19 @@
             for b in range(W)
         ]
         tops = [
-            jnp.where(allowed[b], jnp.max(scores[b], axis=-1, keepdims=True), -FAR) for b in range(W)
+            jnp.where(
+                allowed[b],
+                functools.reduce(
+                    jnp.maximum, [scores[b][:, lanes(n)] for n in range(scores[b].shape[1] // HD)]
+                ),
+                -FAR,
+            )
+            for b in range(W)
         ]
-        top = functools.reduce(jnp.maximum, tops)
+        top = jnp.max(functools.reduce(jnp.maximum, tops), axis=-1, keepdims=True)
         total = None
         for b in range(W):
-            weights = jnp.exp2((scores[b] - jnp.where(allowed[b], top, FAR)) * SCALE)
+            weights = jnp.exp((scores[b] - jnp.where(allowed[b], top, FAR)) * SCALE)
             term = jnp.dot(
                 weights.astype(jnp.bfloat16), value_ref[start + b], preferred_element_type=jnp.float32
             )
@@ -118,6 +151,7 @@
         jnp.int32, (ROWS * GROUPS, HD), 1
     )
     blocks_of = tile // ROWS
+    writes = []
     for i in frames:
         frame = plane * SLOTS + i
         offset = lax.rem(frame + phase, W)
@@ -133,22 +167,21 @@
 
         gate = gate_of(pl.ds(pl.multiple_of(slot * HD, HD), HD))
         gate_shared = gate_of(pl.ds(SLOTS * HD, HD))
-        to = (i - frames[0] + first_out) * GROUPS
-
-        def step(n, carry):
-            query = queries[pl.ds(i * GROUPS + n * blocks_of, blocks_of), 0:ROWS, :].reshape(tile, HD)
+        to = (i - frames[0]) * GROUPS
+
+        for n in range(ROWS * GROUPS // tile):
+            first = i * GROUPS + n * blocks_of
+            query = queries[first : first + blocks_of, 0:ROWS, :].reshape(tile, HD)
             _, numer, total = softmaxed(query, key_all, value_all, start, allowed)
             done = (numer / total * gate).astype(jnp.bfloat16).reshape(blocks_of, ROWS, HD)
-            out[pl.ds(to + n * blocks_of, blocks_of), 0:ROWS, :] = done
-            return carry
-
-        lax.fori_loop(0, ROWS * GROUPS // tile, step, 0)
+            first = to + n * blocks_of
+            out[first : first + blocks_of, 0:ROWS, :] = done
 
         query = queries[i * GROUPS : (i + 1) * GROUPS, ROWS : 2 * ROWS, :].reshape(ROWS * GROUPS, HD)
         top, numer, total = softmaxed(query, key_part, value_part, start, allowed)
         done = (numer / total * gate_shared).astype(jnp.bfloat16).reshape(GROUPS, ROWS, HD)
         out[to : to + GROUPS, ROWS : 2 * ROWS, :] = done
-        weight = top * SCALE + jnp.log(total) * LOG2E
+        weight = top * SCALE + jnp.log(total)
         weight = jnp.where(spot, weight, 0.0).reshape(GROUPS, ROWS, HD).sum(axis=1)
         high = weight.astype(jnp.bfloat16).astype(jnp.float32)
         rest = weight - high
@@ -158,6 +191,15 @@
             at = slice(t, t + 1)
             three = jnp.where(row == 0, high[at], jnp.where(row == 1, middle[at], low[at]))
             out[to + t, 2 * ROWS : O_ROWS, :] = three.astype(jnp.bfloat16)
+        write = pltpu.make_async_copy(
+            out.at[pl.ds(to, GROUPS)],
+            out_ref.at[pl.ds(to + first_out * GROUPS, GROUPS)],
+            sems.at[i - frames[0]],
+        )
+        write.start()
+        writes.append(write)
+    for write in writes:
+        write.wait()
 
 
 def combine_kernel(parts, residual, incoming, out):
@@ -172,7 +214,7 @@
         sent = parts[:, 2 * ROWS : O_ROWS, :].astype(jnp.float32)
         row = lax.broadcasted_iota(jnp.int32, sent.shape, 1)
         weight = jnp.sum(jnp.where(row < 3, sent, 0.0), axis=1).reshape(SLOTS, GROUPS, HD)
-        weight = jnp.exp2(weight - jnp.max(weight, axis=0, keepdims=True))
+        weight = jnp.exp(weight - jnp.max(weight, axis=0, keepdims=True))
         weight = weight / jnp.sum(weight, axis=0, keepdims=True)
         weight = weight.reshape(SLOTS * GROUPS, HD)
         weight = jnp.concatenate([weight, jnp.zeros((HD - SLOTS * GROUPS, HD), jnp.float32)])
@@ -201,19 +243,33 @@
     smem = pl.BlockSpec(memory_space=pltpu.SMEM)
     dests = SLOTS * GROUPS
     exchange = lambda x: lax.all_to_all(x, ("slot", "group"), 0, 0, tiled=True)
-    up = [(z, (z + 1) % planes) for z in range(planes)]
-    down = [(z, (z - 1) % planes) for z in range(planes)]
+    up = [(z, z + 1) for z in range(planes - 1)]
+    down = [(z + 1, z) for z in range(planes - 1)]
     count = planes * SLOTS
 
     kv = pl.pallas_call(
         pack_kv_kernel,
         out_shape=jax.ShapeDtypeStruct((dests, KV_ROWS, HD), jnp.bfloat16),
-        in_specs=whole(3),
-        out_specs=whole(1)[0],
-        compiler_params=params(),
+        in_specs=[HBM, HBM] + whole(1),
+        out_specs=HBM,
+        scratch_shapes=[
+            VMEM(keys.shape[1:], jnp.bfloat16),
+            VMEM(keys.shape[1:], jnp.bfloat16),
+            VMEM((dests, KV_ROWS, HD), jnp.bfloat16),
+            pltpu.SemaphoreType.DMA((2 * ROWS // CHUNK,)),
+            pltpu.SemaphoreType.DMA((SLOTS,)),
+        ],
+        compiler_params=params(62),
+        cost_estimate=pl.CostEstimate(flops=1_000_000, bytes_accessed=40_000_000, transcendentals=0),
         name="pack_kv",
     )(keys[0], values[0], k_gain[None])
     kv = exchange(kv)
+    climbed = lax.ppermute(
+        residual[0],
+        ("plane", "slot"),
+        [(z * SLOTS + SLOTS - 1, (z + 1) * SLOTS + SLOTS - 1) for z in range(planes - 1)],
+    )
+    queries, climbed = lax.optimization_barrier((queries, climbed))
     packed = pl.pallas_call(
         pack_q_kernel,
         out_shape=jax.ShapeDtypeStruct((dests, Q_ROWS, HD), jnp.bfloat16),
@@ -223,10 +279,12 @@
         name="pack_q",
     )(levels, queries[0], q_gain[None])
     query = exchange(packed)
+    shifted = jnp.where(lax.axis_index("slot") == SLOTS - 1, climbed, residual[0])
+    query, shifted = lax.optimization_barrier((query, shifted))
+    moved = lax.ppermute(shifted, "slot", [(i, (i + 1) % SLOTS) for i in range(SLOTS)])
     edge = REACH * GROUPS
     right = lax.ppermute(kv[:edge], "plane", down)
     left = lax.ppermute(kv[dests - edge :], "plane", up)
-    moved = lax.ppermute(residual[0], ("plane", "slot"), [(f, (f + 1) % count) for f in range(count)])
 
     def attend(frames, first_out, slots_out, name):
         blocks = 2 * REACH + SLOTS
@@ -235,12 +293,14 @@
             functools.partial(attend_kernel, frames, first_out, planes, 256),
             out_shape=jax.ShapeDtypeStruct((slots_out * GROUPS, O_ROWS, HD), jnp.bfloat16),
             in_specs=[smem] + whole(5),
-            out_specs=whole(1)[0],
+            out_specs=HBM,
             scratch_shapes=[
                 VMEM((blocks, ROWS * GROUPS, HD), jnp.bfloat16),
                 VMEM((blocks, ROWS * GROUPS, 2 * HD), jnp.bfloat16),
                 VMEM((blocks, PART * GROUPS, HD), jnp.bfloat16),
                 VMEM((blocks, PART * GROUPS, 2 * HD), jnp.bfloat16),
+                VMEM((units * GROUPS, O_ROWS, HD), jnp.bfloat16),
+                pltpu.SemaphoreType.DMA((units,)),
             ],
             compiler_params=params(),
             cost_estimate=pl.CostEstimate(
@@ -249,8 +309,10 @@
             name=name,
         )(offsets, left, kv, right, query, gate_table)
 
-    last = lax.ppermute(attend((SLOTS - 1,), 0, 1, "attend_last"), "plane", up)
+    last = attend((SLOTS - 1,), 0, 1, "attend_last")
+    last = lax.ppermute(last, "plane", up)
     others = attend(tuple(range(SLOTS - 1)), 1, SLOTS, "attend_others")
+    others, moved = lax.optimization_barrier((others, moved))
     parts = exchange(lax.dynamic_update_slice(others, last, (0, 0, 0)))
     updated = pl.pallas_call(
         combine_kernel,

time: 118 us -> 104 us (0.88)
  blocking collectives: 0 us -> 27.6 us
  waiting for transfers between devices: 50 us -> 28.4 us
  starting transfers between devices: 39.4 us -> 26.5 us
  Pallas kernels: 20.4 us -> 16.1 us
  local copies, waits for them, and re-layouts: 5.84 us -> 2.24 us
    all_to_all x0 -> x1, blocking collectives: none -> 27.6 us  [on_device(): exchange = lambda x: lax.all_to_all(x, ('slot', 'group'), 0, 0, tiled=True)]
    ppermute x2 -> x3, waiting for transfers between devices: 16.7 us -> 0.01 us  [the longest x1 0.01 us: on_device(): lax.ppermute(residual[0], ('plane', 'slot'), [(z * SLOTS + SLOTS - 1, (z...]
    all_to_all x3 -> x2, starting transfers between devices: 22.8 us -> 14.6 us  [on_device(): exchange = lambda x: lax.all_to_all(x, ('slot', 'group'), 0, 0, tiled=True)]
    ppermute x1, starting transfers between devices: 9.24 us -> 1.41 us  [on_device(): right = lax.ppermute(kv[:edge], 'plane', down)]
    ppermute x1, waiting for transfers between devices: 6.52 us -> 0.01 us  [on_device(): left = lax.ppermute(kv[dests - edge:], 'plane', up)]
    pallas_call x2, Pallas kernels: 17.2 us -> 10.7 us  [attend(): pl.pallas_call(functools.partial(attend_kernel, frames, first_out, planes...]
    ppermute x1, starting transfers between devices: 1.91 us -> 4.85 us  [on_device(): left = lax.ppermute(kv[dests - edge:], 'plane', up)]
    unnamed x18, local copies, waits for them, and re-layouts: 3.97 us -> 1.06 us
  transfers between devices with their start and end apart: 7 -> 7, of which waited for: 6 -> 2; matrix products, arithmetic and copies ran while one was open for 1% -> 2% of each run, Pallas kernels for 11% -> 11%
where the time goes in v1:
time: 104 us; the launch traced here: 103 us
  waiting for transfers between devices  28.4 us (27%)
  blocking collectives  27.6 us (27%)
  starting transfers between devices  26.5 us (25%)
  Pallas kernels  16.1 us (15%)
  local copies, waits for them, and re-layouts  2.24 us (2%)
  between operations  1.53 us (1%)
    all_to_all x2, waiting for transfers between devices, on_device(): exchange = lambda x: lax.all_to_all(x, ('slot', 'group'), 0, 0, tiled=True)  28.3 us
    all_to_all x1, blocking collectives, on_device(): exchange = lambda x: lax.all_to_all(x, ('slot', 'group'), 0, 0, tiled=True)  27.6 us
    all_to_all x2, starting transfers between devices, on_device(): exchange = lambda x: lax.all_to_all(x, ('slot', 'group'), 0, 0, tiled=True)  14.6 us
    pallas_call x2, Pallas kernels, attend(): pl.pallas_call(functools.partial(attend_kernel, frames, first_out, planes...  10.7 us
    ppermute x1, starting transfers between devices, on_device(): left = lax.ppermute(kv[dests - edge:], 'plane', up)  4.85 us
    pallas_call x1, Pallas kernels, on_device(): pl.pallas_call(pack_kv_kernel, out_shape=jax.ShapeDtypeStruct((dests, KV_...  3.52 us
    ppermute x1, starting transfers between devices, on_device(): last = lax.ppermute(last, 'plane', up)  2.97 us
  transfers between devices with their start and end apart: 7, of which 2 were waited for; matrix products, arithmetic and copies ran while one was open for 2% of the time, Pallas kernels for 11%

profile of v1, /device:TPU:1, one launch (start us, length us, event | category | flops | bytes accessed | tf_op | source)
XLA Modules:
  0.0 103.1 jit_solution(2226638968508170601)
XLA Ops:
  0.0 3.5 %pack_kv.1 = bf16[32,160,128]{2,1,0:T(8,128)(2,1)} custom-call(bf16[64,5120]{1,0:T(8,128)(2,1)} %bitcast.10, bf16[64,5120]{1,0:T(8,128)(2,1)} %bitcast.11, f32[1,5120]{1,0:T(1,128)} %bitcast.13), custom_call_target="tpu_custom_call" | custom-call | flops 1000000 | bytes 40000000 | tf_op jit(solution)/shard_map/pack_kv/pallas_call | solution.py:250
  3.5 0.0 copy-start.5
  3.5 0.0 copy-start.1
  3.6 0.0 copy-start.4
  3.6 10.7 %all-to-all-start = ((bf16[32,160,128]{2,1,0:T(8,128)(2,1)}), bf16[32,160,128]{2,1,0:T(8,128)(2,1)S(1)}, u32[]{:S(2)}, u32[]{:S(2)}) async-start(bf16[32,160,128]{2,1,0:T(8,128)(2,1)} %pack_kv.1), calls=%async_computation | async-start | bytes 2621440 | tf_op jit(solution)/shard_map/all_to_all | solution.py:245
  14.3 0.7 collective-permute-start.2
  15.6 0.0 collective-permute-done.2
  15.6 0.0 copy-start.7
  15.6 0.0 copy-done.1
  15.6 0.0 copy-done.4
  15.7 0.3 pack_q.1
  16.0 0.0 copy-start
  16.0 1.0 copy-done
  17.0 17.7 %all-to-all-done.mine = bf16[32,160,128]{2,1,0:T(8,128)(2,1)S(1)} async-done(((bf16[32,160,128]{2,1,0:T(8,128)(2,1)}), bf16[32,160,128]{2,1,0:T(8,128)(2,1)S(1)}, u32[]{:S(2)}, u32[]{:S(2)}) %all-to-all-start) | async-done | bytes 1310752 | tf_op jit(solution)/shard_map/all_to_all | solution.py:245
  34.7 4.0 %all-to-all-start.1 = ((bf16[32,144,128]{2,1,0:T(8,128)(2,1)}), bf16[32,144,128]{2,1,0:T(8,128)(2,1)S(1)}, u32[]{:S(2)}, u32[]{:S(2)}) async-start(bf16[32,144,128]{2,1,0:T(8,128)(2,1)} %copy-done), calls=%async_computation.1 | async-start | bytes 2359296 | tf_op jit(solution)/shard_map/all_to_all | solution.py:245
  38.7 0.0 copy-start.6
  38.7 1.1 %fusion = (bf16[16,160,128]{2,1,0:T(8,128)(2,1)}, bf16[16,160,128]{2,1,0:T(8,128)(2,1)}) fusion(bf16[32,160,128]{2,1,0:T(8,128)(2,1)S(1)} %all-to-all-done.mine), kind=kLoop, calls=%fused_computation.2 | loop fusion | bytes 2621440 | tf_op jit(solution)/shard_map/slice | solution.py:286
  39.8 1.4 %collective-permute-start.1 = (bf16[16,160,128]{2,1,0:T(8,128)(2,1)}, bf16[16,160,128]{2,1,0:T(8,128)(2,1)S(1)}, u32[]{:S(2)}, u32[]{:S(2)}) collective-permute-start(bf16[16,160,128]{2,1,0:T(8,128)(2,1)} %get-tuple-element.17), channel_id=1, source_target_pairs={{32,0},{64,32},{96,64},{128,96},{160,128},{192,160},{224,192},{256... | collective-permute-start | bytes 1966088 | tf_op jit(solution)/shard_map/ppermute | solution.py:286
  41.2 4.8 %collective-permute-start = (bf16[16,160,128]{2,1,0:T(8,128)(2,1)}, bf16[16,160,128]{2,1,0:T(8,128)(2,1)}, u32[]{:S(2)}, u32[]{:S(2)}) collective-permute-start(bf16[16,160,128]{2,1,0:T(8,128)(2,1)} %get-tuple-element.18), channel_id=1, source_target_pairs={{0,32},{32,64},{64,96},{96,128},{128,160},{160,192},{192,224},{224... | collective-permute-start | bytes 1966088 | tf_op jit(solution)/shard_map/ppermute | solution.py:287
  46.1 0.9 broadcast_select_fusion
  47.0 10.7 %all-to-all-done.1.queries = bf16[32,144,128]{2,1,0:T(8,128)(2,1)S(1)} async-done(((bf16[32,144,128]{2,1,0:T(8,128)(2,1)}), bf16[32,144,128]{2,1,0:T(8,128)(2,1)S(1)}, u32[]{:S(2)}, u32[]{:S(2)}) %all-to-all-start.1) | async-done | bytes 1179680 | tf_op jit(solution)/shard_map/all_to_all | solution.py:245
  57.7 1.9 %collective-permute-start.3 = (bf16[64,5120]{1,0:T(8,128)(2,1)}, bf16[64,5120]{1,0:T(8,128)(2,1)S(1)}, u32[]{:S(2)}, u32[]{:S(2)}) collective-permute-start(bf16[64,5120]{1,0:T(8,128)(2,1)} %broadcast_select_fusion), channel_id=1, source_target_pairs={{0,8},{8,16},{16,24},{24,0},{1,9},{9,17},{17,25},{25,1},{2,10},{10... | collective-permute-start | bytes 1966088 | tf_op jit(solution)/shard_map/ppermute | solution.py:284
  60.2 0.0 collective-permute-done.1.right
  60.2 0.0 collective-permute-done.left
  60.3 3.1 %attend_last.1 = bf16[8,144,128]{2,1,0:T(8,128)(2,1)S(1)} custom-call(s32[1]{0:T(128)S(6)} %copy.13.offsets, bf16[16,160,128]{2,1,0:T(8,128)(2,1)} %collective-permute-done.left, bf16[32,160,128]{2,1,0:T(8,128)(2,1)S(1)} %all-to-all-done.mine, bf16[16,160,128]{2,1,0:T(8,128)(2,1)S(1)} %collective-permute-done.1.right, ...), custom_call_target="tpu_custom_call" | custom-call | flops 500000000 | bytes 4000000 | tf_op jit(solution)/shard_map/attend_last/pallas_call | solution.py:292
  63.4 3.0 %collective-permute-start.4 = (bf16[8,144,128]{2,1,0:T(8,128)(2,1)S(1)}, bf16[8,144,128]{2,1,0:T(8,128)(2,1)S(1)}, u32[]{:S(2)}, u32[]{:S(2)}) collective-permute-start(bf16[8,144,128]{2,1,0:T(8,128)(2,1)S(1)} %attend_last.1), channel_id=1, source_target_pairs={{0,32},{32,64},{64,96},{96,128},{128,160},{160,192},{192,224},{224... | collective-permute-start | bytes 884744 | tf_op jit(solution)/shard_map/ppermute | solution.py:313
  66.4 7.6 %attend_others.1 = bf16[32,144,128]{2,1,0:T(8,128)(2,1)S(1)} custom-call(s32[1]{0:T(128)S(6)} %copy.13.offsets, bf16[16,160,128]{2,1,0:T(8,128)(2,1)} %collective-permute-done.left, bf16[32,160,128]{2,1,0:T(8,128)(2,1)S(1)} %all-to-all-done.mine, bf16[16,160,128]{2,1,0:T(8,128)(2,1)S(1)} %collective-permute-done.1.right, ...), custom_call_target="tpu_custom_call" | custom-call | flops 1500000000 | bytes 4000000 | tf_op jit(solution)/shard_map/attend_others/pallas_call | solution.py:292
  74.0 0.0 collective-permute-done.3.residual
  74.0 0.0 collective-permute-done.4
  74.1 0.0 copy-start.2
  74.1 27.6 %all_to_all.15.parts = bf16[32,144,128]{2,1,0:T(8,128)(2,1)S(1)} all-to-all(bf16[32,144,128]{2,1,0:T(8,128)(2,1)S(1)} %constant_dynamic-update-slice_fusion), channel_id=1, replica_groups=mesh['plane'=16,'slot'=4,'group'=8] {'slot','group'}, dimensions={0} | all-to-all | bytes 2359296 | tf_op jit(solution)/shard_map/all_to_all | solution.py:245
  101.7 1.5 %combine.1 = bf16[64,5120]{1,0:T(8,128)(2,1)} custom-call(bf16[32,144,128]{2,1,0:T(8,128)(2,1)S(1)} %all_to_all.15.parts, bf16[64,5120]{1,0:T(8,128)(2,1)S(1)} %collective-permute-done.3.residual, bf16[64,5120]{1,0:T(8,128)(2,1)S(1)} %copy-done.2), custom_call_target="tpu_custom_call" | custom-call | tf_op jit(solution)/shard_map/combine/pallas_call | solution.py:317
  (9 shorter events, 0.1 us)
Async XLA Ops:
  3.5 10.7 %copy-start.5 = (bf16[1,64,5120]{2,1,0:T(8,128)(2,1)S(1)}, bf16[1,64,5120]{2,1,0:T(8,128)(2,1)}, u32[]{:S(2)}) copy-start(bf16[1,64,5120]{2,1,0:T(8,128)(2,1)} %param.13) | copy-start | bytes 1966084
  3.5 12.1 %copy-start.1 = (bf16[1,64,5120]{2,1,0:T(8,128)(2,1)S(1)}, bf16[1,64,5120]{2,1,0:T(8,128)(2,1)}, u32[]{:S(2)}) copy-start(bf16[1,64,5120]{2,1,0:T(8,128)(2,1)} %param.10) | copy-start | bytes 1966084
  3.6 12.1 %copy-start.4 = (f32[5120]{0:T(1024)S(1)}, f32[5120]{0:T(1024)}, u32[]{:S(2)}) copy-start(f32[5120]{0:T(1024)} %param.14) | copy-start | bytes 61444
  3.6 31.1 %all-to-all-start = ((bf16[32,160,128]{2,1,0:T(8,128)(2,1)}), bf16[32,160,128]{2,1,0:T(8,128)(2,1)S(1)}, u32[]{:S(2)}, u32[]{:S(2)}) async-start(bf16[32,160,128]{2,1,0:T(8,128)(2,1)} %pack_kv.1), calls=%async_computation | async-start | bytes 2621440 | tf_op jit(solution)/shard_map/all_to_all | solution.py:245
  14.3 1.4 %collective-permute-start.2 = (bf16[64,5120]{1,0:T(8,128)(2,1)S(1)}, bf16[64,5120]{1,0:T(8,128)(2,1)S(1)}, u32[]{:S(2)}, u32[]{:S(2)}) collective-permute-start(bf16[64,5120]{1,0:T(8,128)(2,1)S(1)} %bitcast.12), channel_id=1, source_target_pairs={{24,56},{56,88},{88,120},{120,152},{152,184},{184,216},{216,248},{... | collective-permute-start | bytes 1966088 | tf_op jit(solution)/shard_map/ppermute | solution.py:267
  15.6 19.0 %copy-start.7 = (bf16[64,5120]{1,0:T(8,128)(2,1)}, bf16[64,5120]{1,0:T(8,128)(2,1)S(1)}, u32[]{:S(2)}) copy-start(bf16[64,5120]{1,0:T(8,128)(2,1)S(1)} %collective-permute-done.2) | copy-start | bytes 1966084
  16.0 1.0 copy-start
  34.7 23.0 %all-to-all-start.1 = ((bf16[32,144,128]{2,1,0:T(8,128)(2,1)}), bf16[32,144,128]{2,1,0:T(8,128)(2,1)S(1)}, u32[]{:S(2)}, u32[]{:S(2)}) async-start(bf16[32,144,128]{2,1,0:T(8,128)(2,1)} %copy-done), calls=%async_computation.1 | async-start | bytes 2359296 | tf_op jit(solution)/shard_map/all_to_all | solution.py:245
  38.7 7.4 %copy-start.6 = (bf16[1,64,5120]{2,1,0:T(8,128)(2,1)S(1)}, bf16[1,64,5120]{2,1,0:T(8,128)(2,1)}, u32[]{:S(2)}) copy-start(bf16[1,64,5120]{2,1,0:T(8,128)(2,1)} %param.13) | copy-start | bytes 1966084
  38.7 7.4 %copy-start.8 = (bf16[64,5120]{1,0:T(8,128)(2,1)S(1)}, bf16[64,5120]{1,0:T(8,128)(2,1)}, u32[]{:S(2)}) copy-start(bf16[64,5120]{1,0:T(8,128)(2,1)} %copy-done.7) | copy-start | bytes 1966084
  39.8 20.4 %copy-start.3 = (f32[128,640]{1,0:T(8,128)S(1)}, f32[128,640]{1,0:T(8,128)}, u32[]{:S(2)}) copy-start(f32[128,640]{1,0:T(8,128)} %gates.3) | copy-start | bytes 983044
  39.8 20.4 %collective-permute-start.1 = (bf16[16,160,128]{2,1,0:T(8,128)(2,1)}, bf16[16,160,128]{2,1,0:T(8,128)(2,1)S(1)}, u32[]{:S(2)}, u32[]{:S(2)}) collective-permute-start(bf16[16,160,128]{2,1,0:T(8,128)(2,1)} %get-tuple-element.17), channel_id=1, source_target_pairs={{32,0},{64,32},{96,64},{128,96},{160,128},{192,160},{224,192},{256... | collective-permute-start | bytes 1966088 | tf_op jit(solution)/shard_map/ppermute | solution.py:286
  41.2 19.0 %collective-permute-start = (bf16[16,160,128]{2,1,0:T(8,128)(2,1)}, bf16[16,160,128]{2,1,0:T(8,128)(2,1)}, u32[]{:S(2)}, u32[]{:S(2)}) collective-permute-start(bf16[16,160,128]{2,1,0:T(8,128)(2,1)} %get-tuple-element.18), channel_id=1, source_target_pairs={{0,32},{32,64},{64,96},{96,128},{128,160},{160,192},{192,224},{224... | collective-permute-start | bytes 1966088 | tf_op jit(solution)/shard_map/ppermute | solution.py:287
  57.7 16.3 %collective-permute-start.3 = (bf16[64,5120]{1,0:T(8,128)(2,1)}, bf16[64,5120]{1,0:T(8,128)(2,1)S(1)}, u32[]{:S(2)}, u32[]{:S(2)}) collective-permute-start(bf16[64,5120]{1,0:T(8,128)(2,1)} %broadcast_select_fusion), channel_id=1, source_target_pairs={{0,8},{8,16},{16,24},{24,0},{1,9},{9,17},{17,25},{25,1},{2,10},{10... | collective-permute-start | bytes 1966088 | tf_op jit(solution)/shard_map/ppermute | solution.py:284
  63.4 10.6 %collective-permute-start.4 = (bf16[8,144,128]{2,1,0:T(8,128)(2,1)S(1)}, bf16[8,144,128]{2,1,0:T(8,128)(2,1)S(1)}, u32[]{:S(2)}, u32[]{:S(2)}) collective-permute-start(bf16[8,144,128]{2,1,0:T(8,128)(2,1)S(1)} %attend_last.1), channel_id=1, source_target_pairs={{0,32},{32,64},{64,96},{96,128},{128,160},{160,192},{192,224},{224... | collective-permute-start | bytes 884744 | tf_op jit(solution)/shard_map/ppermute | solution.py:313
  74.1 27.6 %copy-start.2 = (bf16[64,5120]{1,0:T(8,128)(2,1)S(1)}, bf16[64,5120]{1,0:T(8,128)(2,1)}, u32[]{:S(2)}) copy-start(bf16[64,5120]{1,0:T(8,128)(2,1)} %incoming.1) | copy-start | bytes 1966084

commit v2 on v1

--- a/solution.py
+++ b/solution.py
@@ -15,11 +15,10 @@
 OWN = 5
 ROWS = 64
 PART = ROWS // SLOTS
-CHUNK = 16
 KV_ROWS = 2 * (ROWS + PART)
 Q_ROWS = 2 * ROWS + 16
 O_ROWS = 2 * ROWS + 16
-SCALE = 1.0 / math.sqrt(HD)
+SCALE = math.log2(math.e) / math.sqrt(HD)
 FAR = 1e30
 VMEM = pltpu.VMEM
 HBM = pl.BlockSpec(memory_space=pltpu.HBM)
@@ -38,43 +37,33 @@
 
 
 def pack_kv_kernel(keys_in, values_in, gain, out, keys, values, blocks, in_sems, out_sems):
-    chunks = ROWS // CHUNK
-    reads = []
-    for n, (source, target) in enumerate(((keys_in, keys), (values_in, values))):
-        for c in range(chunks):
-            at = pl.ds(c * CHUNK, CHUNK)
-            read = pltpu.make_async_copy(source.at[at], target.at[at], in_sems.at[n * chunks + c])
-            read.start()
-            reads.append(read)
-    scales = []
-    for c in range(chunks):
-        reads[c].wait()
-        scales.append(scale_of(keys[c * CHUNK : (c + 1) * CHUNK, :].astype(jnp.float32)))
-    by = jnp.concatenate(scales)
-    for read in reads[chunks:]:
-        read.wait()
-
-    def pair(head):
-        at = lanes(head)
-        key = (keys[:, at].astype(jnp.float32) * by * gain[:, at]).astype(jnp.bfloat16)
-        return key, values[:, at]
-
-    for group in range(GROUPS):
-        key, value = pair(group * OWN + SLOTS)
+    reads = [
+        pltpu.make_async_copy(source, target, in_sems.at[n])
+        for n, (source, target) in enumerate(((values_in, values), (keys_in, keys)))
+    ]
+    for read in reads:
+        read.start()
+    writes = []
+
+    def spread(make, base):
+        for group in range(GROUPS):
+            block = make(lanes(group * OWN + SLOTS))
+            for slot in range(SLOTS):
+                part = slice(slot * PART, (slot + 1) * PART)
+                blocks[slot * GROUPS + group, base + ROWS : base + ROWS + PART, :] = block[part]
         for slot in range(SLOTS):
-            part = slice(slot * PART, (slot + 1) * PART)
-            blocks[slot * GROUPS + group, ROWS : ROWS + PART, :] = key[part]
-            blocks[slot * GROUPS + group, 2 * ROWS + PART : KV_ROWS, :] = value[part]
-    writes = []
-    for slot in range(SLOTS):
-        for group in range(GROUPS):
-            key, value = pair(group * OWN + slot)
-            blocks[slot * GROUPS + group, 0:ROWS, :] = key
-            blocks[slot * GROUPS + group, ROWS + PART : 2 * ROWS + PART, :] = value
-        at = pl.ds(slot * GROUPS, GROUPS)
-        write = pltpu.make_async_copy(blocks.at[at], out.at[at], out_sems.at[slot])
-        write.start()
-        writes.append(write)
+            for group in range(GROUPS):
+                blocks[slot * GROUPS + group, base : base + ROWS, :] = make(lanes(group * OWN + slot))
+            at = pl.ds(slot * GROUPS, GROUPS), pl.ds(base, ROWS + PART)
+            write = pltpu.make_async_copy(blocks.at[at], out.at[at], out_sems.at[len(writes)])
+            write.start()
+            writes.append(write)
+
+    reads[0].wait()
+    spread(lambda at: values[:, at], ROWS + PART)
+    reads[1].wait()
+    by = scale_of(keys[...].astype(jnp.float32))
+    spread(lambda at: (keys[:, at].astype(jnp.float32) * by * gain[:, at]).astype(jnp.bfloat16), 0)
     for write in writes:
         write.wait()
 
@@ -95,16 +84,27 @@
 
 
 def attend_kernel(
-    frames, first_out, planes, tile, offsets, left, mine, right, queries, gates, out_ref, key_all, value_all, key_part, value_part, out, sems
+    frames, first_out, planes, tile, offsets, mine, right, queries, gates, left_in, out_ref, key_all, value_all, key_part, value_part, out, sems, left, left_sem
 ):
     plane = lax.axis_index("plane")
     slot = lax.axis_index("slot")
     count = planes * SLOTS
     phase = lax.rem(offsets[0] + W * count - (plane * SLOTS + slot), W)
-    blocks = 2 * REACH + SLOTS
     ones = jnp.ones((ROWS * GROUPS, HD), jnp.bfloat16)
-    for j in range(min(frames), max(frames) + 2 * REACH + 1):
+    below = None
+    if left_in is not None:
+        below = pltpu.make_async_copy(left_in, left, left_sem.at[0])
+        below.start()
+    unpacked = set()
+
+    def unpack(j):
+        if j in unpacked:
+            return
+        unpacked.add(j)
         if j < REACH:
+            if not waited:
+                below.wait()
+                waited.append(True)
             ref, base = left, j * GROUPS
         elif j < REACH + SLOTS:
             ref, base = mine, (j - REACH) * GROUPS
@@ -117,6 +117,8 @@
         value_all[j, :, HD:] = ones
         value_part[j, :, 0:HD] = ref[from_all, 2 * ROWS + PART : KV_ROWS, :].reshape(PART * GROUPS, HD)
         value_part[j, :, HD:] = ones[: PART * GROUPS]
+
+    waited = []
 
     def softmaxed(query, key_ref, value_ref, start, allowed):
         scores = [
@@ -138,7 +140,7 @@
         top = jnp.max(functools.reduce(jnp.maximum, tops), axis=-1, keepdims=True)
         total = None
         for b in range(W):
-            weights = jnp.exp((scores[b] - jnp.where(allowed[b], top, FAR)) * SCALE)
+            weights = jnp.exp2((scores[b] - jnp.where(allowed[b], top, FAR)) * SCALE)
             term = jnp.dot(
                 weights.astype(jnp.bfloat16), value_ref[start + b], preferred_element_type=jnp.float32
             )
@@ -152,7 +154,9 @@
     )
     blocks_of = tile // ROWS
     writes = []
-    for i in frames:
+    for i in reversed(frames):
+        for j in range(i + 2 * REACH, i - 1, -1):
+            unpack(j)
         frame = plane * SLOTS + i
         offset = lax.rem(frame + phase, W)
         start = i + REACH - offset
@@ -181,7 +185,7 @@
         top, numer, total = softmaxed(query, key_part, value_part, start, allowed)
         done = (numer / total * gate_shared).astype(jnp.bfloat16).reshape(GROUPS, ROWS, HD)
         out[to : to + GROUPS, ROWS : 2 * ROWS, :] = done
-        weight = top * SCALE + jnp.log(total)
+        weight = top * SCALE + jnp.log2(total)
         weight = jnp.where(spot, weight, 0.0).reshape(GROUPS, ROWS, HD).sum(axis=1)
         high = weight.astype(jnp.bfloat16).astype(jnp.float32)
         rest = weight - high
@@ -202,23 +206,26 @@
         write.wait()
 
 
-def combine_kernel(parts, residual, incoming, out):
+def combine_kernel(parts, residual, incoming, out_ref, out, sems):
     first = (lax.axis_index("plane") == 0) & (lax.axis_index("slot") == 0)
 
     @pl.when(first)
     def _():
-        out[...] = incoming[...]
+        write = pltpu.make_async_copy(incoming, out_ref, sems.at[0])
+        write.start()
+        write.wait()
 
     @pl.when(jnp.logical_not(first))
     def _():
         sent = parts[:, 2 * ROWS : O_ROWS, :].astype(jnp.float32)
         row = lax.broadcasted_iota(jnp.int32, sent.shape, 1)
         weight = jnp.sum(jnp.where(row < 3, sent, 0.0), axis=1).reshape(SLOTS, GROUPS, HD)
-        weight = jnp.exp(weight - jnp.max(weight, axis=0, keepdims=True))
+        weight = jnp.exp2(weight - jnp.max(weight, axis=0, keepdims=True))
         weight = weight / jnp.sum(weight, axis=0, keepdims=True)
         weight = weight.reshape(SLOTS * GROUPS, HD)
         weight = jnp.concatenate([weight, jnp.zeros((HD - SLOTS * GROUPS, HD), jnp.float32)])
         weight = weight.T[:ROWS]
+        writes = []
         for group in range(GROUPS):
             shared = None
             for slot in range(SLOTS):
@@ -231,6 +238,13 @@
             at = lanes(group * OWN + SLOTS)
             shared = shared.astype(jnp.bfloat16).astype(jnp.float32)
             out[:, at] = (residual[:, at].astype(jnp.float32) + shared).astype(jnp.bfloat16)
+            if group % 2:
+                at = pl.ds((group - 1) * OWN * HD, 2 * OWN * HD)
+                write = pltpu.make_async_copy(out.at[:, at], out_ref.at[:, at], sems.at[group // 2])
+                write.start()
+                writes.append(write)
+        for write in writes:
+            write.wait()
 
 
 def whole(count):
@@ -256,8 +270,8 @@
             VMEM(keys.shape[1:], jnp.bfloat16),
             VMEM(keys.shape[1:], jnp.bfloat16),
             VMEM((dests, KV_ROWS, HD), jnp.bfloat16),
-            pltpu.SemaphoreType.DMA((2 * ROWS // CHUNK,)),
-            pltpu.SemaphoreType.DMA((SLOTS,)),
+            pltpu.SemaphoreType.DMA((2,)),
+            pltpu.SemaphoreType.DMA((2 * SLOTS,)),
         ],
         compiler_params=params(62),
         cost_estimate=pl.CostEstimate(flops=1_000_000, bytes_accessed=40_000_000, transcendentals=0),
@@ -285,14 +299,19 @@
     edge = REACH * GROUPS
     right = lax.ppermute(kv[:edge], "plane", down)
     left = lax.ppermute(kv[dests - edge :], "plane", up)
-
     def attend(frames, first_out, slots_out, name):
         blocks = 2 * REACH + SLOTS
         units = len(frames)
+        below = [left] if min(frames) < REACH else []
+
+        def kernel(*refs):
+            fixed, rest = refs[:5], refs[5:]
+            attend_kernel(frames, first_out, planes, 256, *fixed, *(rest if below else (None, *rest)))
+
         return pl.pallas_call(
-            functools.partial(attend_kernel, frames, first_out, planes, 256),
+            kernel,
             out_shape=jax.ShapeDtypeStruct((slots_out * GROUPS, O_ROWS, HD), jnp.bfloat16),
-            in_specs=[smem] + whole(5),
+            in_specs=[smem] + whole(4) + [HBM] * len(below),
             out_specs=HBM,
             scratch_shapes=[
                 VMEM((blocks, ROWS * GROUPS, HD), jnp.bfloat16),
@@ -301,13 +320,15 @@
                 VMEM((blocks, PART * GROUPS, 2 * HD), jnp.bfloat16),
                 VMEM((units * GROUPS, O_ROWS, HD), jnp.bfloat16),
                 pltpu.SemaphoreType.DMA((units,)),
+                VMEM((edge, KV_ROWS, HD), jnp.bfloat16),
+                pltpu.SemaphoreType.DMA((1,)),
             ],
-            compiler_params=params(),
+            compiler_params=params(32),
             cost_estimate=pl.CostEstimate(
                 flops=units * 500_000_000, bytes_accessed=4_000_000, transcendentals=units * 1_000_000
             ),
             name=name,
-        )(offsets, left, kv, right, query, gate_table)
+        )(offsets, kv, right, query, gate_table, *below)
 
     last = attend((SLOTS - 1,), 0, 1, "attend_last")
     last = lax.ppermute(last, "plane", up)
@@ -318,7 +339,8 @@
         combine_kernel,
         out_shape=jax.ShapeDtypeStruct(incoming.shape, jnp.bfloat16),
         in_specs=whole(3),
-        out_specs=whole(1)[0],
+        out_specs=HBM,
+        scratch_shapes=[VMEM(incoming.shape, jnp.bfloat16), pltpu.SemaphoreType.DMA((GROUPS // 2,))],
         compiler_params=params(),
         name="combine",
     )(parts, moved, incoming)

time: 104 us -> 97.8 us (0.940)
  blocking collectives: 27.6 us -> 25.3 us
  Pallas kernels: 16.1 us -> 14.1 us
  starting transfers between devices: 26.5 us -> 25.2 us
    pallas_call x2, Pallas kernels: 10.7 us -> 8.26 us  [attend(): pl.pallas_call(kernel, out_shape=jax.ShapeDtypeStruct((slots_out * GROUPS...]
    all_to_all x1, blocking collectives: 27.6 us -> 25.3 us  [on_device(): exchange = lambda x: lax.all_to_all(x, ('slot', 'group'), 0, 0, tiled=True)]
    ppermute x1, starting transfers between devices: 2.97 us -> 1.68 us  [on_device(): last = lax.ppermute(last, 'plane', up)]
  transfers between devices with their start and end apart: 7 -> 7, of which waited for: 2 -> 2; matrix products, arithmetic and copies ran while one was open for 2% -> 2% of each run, Pallas kernels for 11% -> 10%
where the time goes in v2:
time: 97.8 us; the launch traced here: 96.6 us
  waiting for transfers between devices  28.4 us (29%)
  blocking collectives  25.3 us (26%)
  starting transfers between devices  25.2 us (26%)
  Pallas kernels  14.1 us (14%)
  between operations  1.51 us (2%)
  local copies, waits for them, and re-layouts  1.23 us (1%)
    all_to_all x2, waiting for transfers between devices, on_device(): exchange = lambda x: lax.all_to_all(x, ('slot', 'group'), 0, 0, tiled=True)  28.3 us
    all_to_all x1, blocking collectives, on_device(): exchange = lambda x: lax.all_to_all(x, ('slot', 'group'), 0, 0, tiled=True)  25.3 us
    all_to_all x2, starting transfers between devices, on_device(): exchange = lambda x: lax.all_to_all(x, ('slot', 'group'), 0, 0, tiled=True)  14.6 us
    pallas_call x2, Pallas kernels, attend(): pl.pallas_call(kernel, out_shape=jax.ShapeDtypeStruct((slots_out * GROUPS...  8.26 us
    ppermute x1, starting transfers between devices, on_device(): left = lax.ppermute(kv[dests - edge:], 'plane', up)  4.85 us
    pallas_call x1, Pallas kernels, on_device(): pl.pallas_call(pack_kv_kernel, out_shape=jax.ShapeDtypeStruct((dests, KV_...  3.21 us
  transfers between devices with their start and end apart: 7, of which 2 were waited for; matrix products, arithmetic and copies ran while one was open for 2% of the time, Pallas kernels for 10%

profile of v2, /device:TPU:1, one launch (start us, length us, event | category | flops | bytes accessed | tf_op | source)
XLA Modules:
  0.0 96.6 jit_solution(15223312248540340433)
XLA Ops:
  0.0 3.2 %pack_kv.1 = bf16[32,160,128]{2,1,0:T(8,128)(2,1)} custom-call(bf16[64,5120]{1,0:T(8,128)(2,1)} %bitcast.10, bf16[64,5120]{1,0:T(8,128)(2,1)} %bitcast.11, f32[1,5120]{1,0:T(1,128)} %bitcast.13), custom_call_target="tpu_custom_call" | custom-call | flops 1000000 | bytes 40000000 | tf_op jit(solution)/shard_map/pack_kv/pallas_call | solution.py:264
  3.2 0.0 copy-start.4
  3.2 0.0 copy-start
  3.2 0.0 copy-start.3
  3.3 10.7 %all-to-all-start = ((bf16[32,160,128]{2,1,0:T(8,128)(2,1)}), bf16[32,160,128]{2,1,0:T(8,128)(2,1)S(1)}, u32[]{:S(2)}, u32[]{:S(2)}) async-start(bf16[32,160,128]{2,1,0:T(8,128)(2,1)} %pack_kv.1), calls=%async_computation | async-start | bytes 2621440 | tf_op jit(solution)/shard_map/all_to_all | solution.py:259
  13.9 0.7 collective-permute-start.1
  15.3 0.0 collective-permute-done.1
  15.3 0.0 copy-start.6
  15.3 0.0 copy-done
  15.3 0.0 copy-done.3
  15.3 1.3 %pack_q.1 = bf16[32,144,128]{2,1,0:T(8,128)(2,1)} custom-call(s32[1]{0:T(128)S(6)} %copy.12.levels, bf16[64,5120]{1,0:T(8,128)(2,1)S(1)} %bitcast.8, f32[1,5120]{1,0:T(1,128)S(1)} %bitcast.9), custom_call_target="tpu_custom_call" | custom-call | tf_op jit(solution)/shard_map/pack_q/pallas_call | solution.py:287
  16.7 17.7 %all-to-all-done.refs_1_ = bf16[32,160,128]{2,1,0:T(8,128)(2,1)S(1)} async-done(((bf16[32,160,128]{2,1,0:T(8,128)(2,1)}), bf16[32,160,128]{2,1,0:T(8,128)(2,1)S(1)}, u32[]{:S(2)}, u32[]{:S(2)}) %all-to-all-start) | async-done | bytes 1310752 | tf_op jit(solution)/shard_map/all_to_all | solution.py:259
  34.4 4.0 %all-to-all-start.1 = ((bf16[32,144,128]{2,1,0:T(8,128)(2,1)}), bf16[32,144,128]{2,1,0:T(8,128)(2,1)S(1)}, u32[]{:S(2)}, u32[]{:S(2)}) async-start(bf16[32,144,128]{2,1,0:T(8,128)(2,1)} %pack_q.1), calls=%async_computation.1 | async-start | bytes 2359296 | tf_op jit(solution)/shard_map/all_to_all | solution.py:259
  38.3 0.0 copy-start.5
  38.4 0.0 copy-start.7
  38.4 1.1 %fusion = (bf16[16,160,128]{2,1,0:T(8,128)(2,1)}, bf16[16,160,128]{2,1,0:T(8,128)(2,1)}) fusion(bf16[32,160,128]{2,1,0:T(8,128)(2,1)S(1)} %all-to-all-done.refs_1_), kind=kLoop, calls=%fused_computation.2 | loop fusion | bytes 2621440 | tf_op jit(solution)/shard_map/slice | solution.py:301
  39.5 1.4 %collective-permute-start = (bf16[16,160,128]{2,1,0:T(8,128)(2,1)}, bf16[16,160,128]{2,1,0:T(8,128)(2,1)S(1)}, u32[]{:S(2)}, u32[]{:S(2)}) collective-permute-start(bf16[16,160,128]{2,1,0:T(8,128)(2,1)} %get-tuple-element.18), channel_id=1, source_target_pairs={{32,0},{64,32},{96,64},{128,96},{160,128},{192,160},{224,192},{256... | collective-permute-start | bytes 1966088 | tf_op jit(solution)/shard_map/ppermute | solution.py:300
  40.9 4.9 %collective-permute-start.2 = (bf16[16,160,128]{2,1,0:T(8,128)(2,1)}, bf16[16,160,128]{2,1,0:T(8,128)(2,1)}, u32[]{:S(2)}, u32[]{:S(2)}) collective-permute-start(bf16[16,160,128]{2,1,0:T(8,128)(2,1)} %get-tuple-element.17), channel_id=1, source_target_pairs={{0,32},{32,64},{64,96},{96,128},{128,160},{160,192},{192,224},{224... | collective-permute-start | bytes 1966088 | tf_op jit(solution)/shard_map/ppermute | solution.py:301
  45.8 0.0 copy-done.7
  45.8 0.9 broadcast_select_fusion
  46.7 10.7 %all-to-all-done.1.refs_3_ = bf16[32,144,128]{2,1,0:T(8,128)(2,1)S(1)} async-done(((bf16[32,144,128]{2,1,0:T(8,128)(2,1)}), bf16[32,144,128]{2,1,0:T(8,128)(2,1)S(1)}, u32[]{:S(2)}, u32[]{:S(2)}) %all-to-all-start.1) | async-done | bytes 1179680 | tf_op jit(solution)/shard_map/all_to_all | solution.py:259
  57.4 1.9 %collective-permute-start.3 = (bf16[64,5120]{1,0:T(8,128)(2,1)}, bf16[64,5120]{1,0:T(8,128)(2,1)S(1)}, u32[]{:S(2)}, u32[]{:S(2)}) collective-permute-start(bf16[64,5120]{1,0:T(8,128)(2,1)} %broadcast_select_fusion), channel_id=1, source_target_pairs={{0,8},{8,16},{16,24},{24,0},{1,9},{9,17},{17,25},{25,1},{2,10},{10... | collective-permute-start | bytes 1966088 | tf_op jit(solution)/shard_map/ppermute | solution.py:298
  59.9 0.0 collective-permute-done.refs_2_
  60.0 2.0 %attend_last.1 = bf16[8,144,128]{2,1,0:T(8,128)(2,1)S(1)} custom-call(s32[1]{0:T(128)S(6)} %copy.13.refs_0_, bf16[32,160,128]{2,1,0:T(8,128)(2,1)S(1)} %all-to-all-done.refs_1_, bf16[16,160,128]{2,1,0:T(8,128)(2,1)S(1)} %collective-permute-done.refs_2_, bf16[32,144,128]{2,1,0:T(8,128)(2,1)S(1)} %all-to-all-done.1.refs_3_, f32[128,640]{1,0:T(8,128)S(1)} %copy-done.2), custom_call_target="tpu_custom_call" | custom-call | flops 500000000 | bytes 4000000 | tf_op jit(solution)/shard_map/attend_last/pallas_call | solution.py:311
  61.9 1.7 %collective-permute-start.4 = (bf16[8,144,128]{2,1,0:T(8,128)(2,1)S(1)}, bf16[8,144,128]{2,1,0:T(8,128)(2,1)S(1)}, u32[]{:S(2)}, u32[]{:S(2)}) collective-permute-start(bf16[8,144,128]{2,1,0:T(8,128)(2,1)S(1)} %attend_last.1), channel_id=1, source_target_pairs={{0,32},{32,64},{64,96},{96,128},{128,160},{160,192},{192,224},{224... | collective-permute-start | bytes 884744 | tf_op jit(solution)/shard_map/ppermute | solution.py:334
  63.6 0.0 collective-permute-done.2.refs_5_
  63.6 6.3 %attend_others.1 = bf16[32,144,128]{2,1,0:T(8,128)(2,1)S(1)} custom-call(s32[1]{0:T(128)S(6)} %copy.13.refs_0_, bf16[32,160,128]{2,1,0:T(8,128)(2,1)S(1)} %all-to-all-done.refs_1_, bf16[16,160,128]{2,1,0:T(8,128)(2,1)S(1)} %collective-permute-done.refs_2_, bf16[32,144,128]{2,1,0:T(8,128)(2,1)S(1)} %all-to-all-done.1.refs_3_, f32[128,640]{1,0:T(8,128)S(1)} %copy-done.2, ...), custom_call_target="tpu_custom_call" | custom-call | flops 1500000000 | bytes 4000000 | tf_op jit(solution)/shard_map/attend_others/pallas_call | solution.py:311
  69.9 0.0 collective-permute-done.3.residual
  69.9 0.0 collective-permute-done.4
  70.0 0.0 copy-start.1
  70.0 25.3 %all_to_all.15.parts = bf16[32,144,128]{2,1,0:T(8,128)(2,1)S(1)} all-to-all(bf16[32,144,128]{2,1,0:T(8,128)(2,1)S(1)} %constant_dynamic-update-slice_fusion), channel_id=1, replica_groups=mesh['plane'=16,'slot'=4,'group'=8] {'slot','group'}, dimensions={0} | all-to-all | bytes 2359296 | tf_op jit(solution)/shard_map/all_to_all | solution.py:259
  95.3 1.3 %combine.1 = bf16[64,5120]{1,0:T(8,128)(2,1)} custom-call(bf16[32,144,128]{2,1,0:T(8,128)(2,1)S(1)} %all_to_all.15.parts, bf16[64,5120]{1,0:T(8,128)(2,1)S(1)} %collective-permute-done.3.residual, bf16[64,5120]{1,0:T(8,128)(2,1)S(1)} %copy-done.1), custom_call_target="tpu_custom_call" | custom-call | tf_op jit(solution)/shard_map/combine/pallas_call | solution.py:338
  (7 shorter events, 0.1 us)
Async XLA Ops:
  3.2 10.7 %copy-start.4 = (bf16[1,64,5120]{2,1,0:T(8,128)(2,1)S(1)}, bf16[1,64,5120]{2,1,0:T(8,128)(2,1)}, u32[]{:S(2)}) copy-start(bf16[1,64,5120]{2,1,0:T(8,128)(2,1)} %param.13) | copy-start | bytes 1966084
  3.2 12.1 %copy-start = (bf16[1,64,5120]{2,1,0:T(8,128)(2,1)S(1)}, bf16[1,64,5120]{2,1,0:T(8,128)(2,1)}, u32[]{:S(2)}) copy-start(bf16[1,64,5120]{2,1,0:T(8,128)(2,1)} %param.10) | copy-start | bytes 1966084
  3.2 12.1 %copy-start.3 = (f32[5120]{0:T(1024)S(1)}, f32[5120]{0:T(1024)}, u32[]{:S(2)}) copy-start(f32[5120]{0:T(1024)} %param.14) | copy-start | bytes 61444
  3.3 31.1 %all-to-all-start = ((bf16[32,160,128]{2,1,0:T(8,128)(2,1)}), bf16[32,160,128]{2,1,0:T(8,128)(2,1)S(1)}, u32[]{:S(2)}, u32[]{:S(2)}) async-start(bf16[32,160,128]{2,1,0:T(8,128)(2,1)} %pack_kv.1), calls=%async_computation | async-start | bytes 2621440 | tf_op jit(solution)/shard_map/all_to_all | solution.py:259
  13.9 1.4 %collective-permute-start.1 = (bf16[64,5120]{1,0:T(8,128)(2,1)S(1)}, bf16[64,5120]{1,0:T(8,128)(2,1)S(1)}, u32[]{:S(2)}, u32[]{:S(2)}) collective-permute-start(bf16[64,5120]{1,0:T(8,128)(2,1)S(1)} %bitcast.12), channel_id=1, source_target_pairs={{24,56},{56,88},{88,120},{120,152},{152,184},{184,216},{216,248},{... | collective-permute-start | bytes 1966088 | tf_op jit(solution)/shard_map/ppermute | solution.py:281
  15.3 19.0 %copy-start.6 = (bf16[64,5120]{1,0:T(8,128)(2,1)}, bf16[64,5120]{1,0:T(8,128)(2,1)S(1)}, u32[]{:S(2)}) copy-start(bf16[64,5120]{1,0:T(8,128)(2,1)S(1)} %collective-permute-done.1) | copy-start | bytes 1966084
  34.4 23.0 %all-to-all-start.1 = ((bf16[32,144,128]{2,1,0:T(8,128)(2,1)}), bf16[32,144,128]{2,1,0:T(8,128)(2,1)S(1)}, u32[]{:S(2)}, u32[]{:S(2)}) async-start(bf16[32,144,128]{2,1,0:T(8,128)(2,1)} %pack_q.1), calls=%async_computation.1 | async-start | bytes 2359296 | tf_op jit(solution)/shard_map/all_to_all | solution.py:259
  38.3 7.4 %copy-start.5 = (bf16[1,64,5120]{2,1,0:T(8,128)(2,1)S(1)}, bf16[1,64,5120]{2,1,0:T(8,128)(2,1)}, u32[]{:S(2)}) copy-start(bf16[1,64,5120]{2,1,0:T(8,128)(2,1)} %param.13) | copy-start | bytes 1966084
  38.4 7.4 %copy-start.7 = (bf16[64,5120]{1,0:T(8,128)(2,1)S(1)}, bf16[64,5120]{1,0:T(8,128)(2,1)}, u32[]{:S(2)}) copy-start(bf16[64,5120]{1,0:T(8,128)(2,1)} %copy-done.6) | copy-start | bytes 1966084
  39.5 20.4 %copy-start.2 = (f32[128,640]{1,0:T(8,128)S(1)}, f32[128,640]{1,0:T(8,128)}, u32[]{:S(2)}) copy-start(f32[128,640]{1,0:T(8,128)} %refs_4_.3) | copy-start | bytes 983044
  39.5 20.4 %collective-permute-start = (bf16[16,160,128]{2,1,0:T(8,128)(2,1)}, bf16[16,160,128]{2,1,0:T(8,128)(2,1)S(1)}, u32[]{:S(2)}, u32[]{:S(2)}) collective-permute-start(bf16[16,160,128]{2,1,0:T(8,128)(2,1)} %get-tuple-element.18), channel_id=1, source_target_pairs={{32,0},{64,32},{96,64},{128,96},{160,128},{192,160},{224,192},{256... | collective-permute-start | bytes 1966088 | tf_op jit(solution)/shard_map/ppermute | solution.py:300
  40.9 22.7 %collective-permute-start.2 = (bf16[16,160,128]{2,1,0:T(8,128)(2,1)}, bf16[16,160,128]{2,1,0:T(8,128)(2,1)}, u32[]{:S(2)}, u32[]{:S(2)}) collective-permute-start(bf16[16,160,128]{2,1,0:T(8,128)(2,1)} %get-tuple-element.17), channel_id=1, source_target_pairs={{0,32},{32,64},{64,96},{96,128},{128,160},{160,192},{192,224},{224... | collective-permute-start | bytes 1966088 | tf_op jit(solution)/shard_map/ppermute | solution.py:301
  57.4 12.6 %collective-permute-start.3 = (bf16[64,5120]{1,0:T(8,128)(2,1)}, bf16[64,5120]{1,0:T(8,128)(2,1)S(1)}, u32[]{:S(2)}, u32[]{:S(2)}) collective-permute-start(bf16[64,5120]{1,0:T(8,128)(2,1)} %broadcast_select_fusion), channel_id=1, source_target_pairs={{0,8},{8,16},{16,24},{24,0},{1,9},{9,17},{17,25},{25,1},{2,10},{10... | collective-permute-start | bytes 1966088 | tf_op jit(solution)/shard_map/ppermute | solution.py:298
  61.9 8.0 %collective-permute-start.4 = (bf16[8,144,128]{2,1,0:T(8,128)(2,1)S(1)}, bf16[8,144,128]{2,1,0:T(8,128)(2,1)S(1)}, u32[]{:S(2)}, u32[]{:S(2)}) collective-permute-start(bf16[8,144,128]{2,1,0:T(8,128)(2,1)S(1)} %attend_last.1), channel_id=1, source_target_pairs={{0,32},{32,64},{64,96},{96,128},{128,160},{160,192},{192,224},{224... | collective-permute-start | bytes 884744 | tf_op jit(solution)/shard_map/ppermute | solution.py:334
  70.0 25.3 %copy-start.1 = (bf16[64,5120]{1,0:T(8,128)(2,1)S(1)}, bf16[64,5120]{1,0:T(8,128)(2,1)}, u32[]{:S(2)}) copy-start(bf16[64,5120]{1,0:T(8,128)(2,1)} %incoming.1) | copy-start | bytes 1966084

commit v3 on v2

--- a/solution.py
+++ b/solution.py
@@ -9,8 +9,9 @@
 
 HD = 128
 W = 3
-REACH = W - 1
 SLOTS = 4
+BELOW = 3
+ABOVE = 1
 GROUPS = 8
 OWN = 5
 ROWS = 64
@@ -68,48 +69,70 @@
         write.wait()
 
 
-def pack_q_kernel(levels, queries, gain, out):
-    by = scale_of(queries[...].astype(jnp.float32))
-    level = jnp.full((16, HD), levels[0], jnp.int32).astype(jnp.float32).astype(jnp.bfloat16)
-    for group in range(GROUPS):
-        for own in range(OWN):
-            at = lanes(group * OWN + own)
-            query = (queries[:, at].astype(jnp.float32) * by * gain[:, at]).astype(jnp.bfloat16)
-            if own < SLOTS:
-                out[own * GROUPS + group, 0:ROWS, :] = query
-                out[own * GROUPS + group, 2 * ROWS : Q_ROWS, :] = level
-            else:
-                for slot in range(SLOTS):
-                    out[slot * GROUPS + group, ROWS : 2 * ROWS, :] = query
+def pack_q_kernel(levels, own, climbed, gain, out):
+    last = lax.axis_index("slot") == SLOTS - 1
+    width = own.shape[1]
+
+    def spread(queries, info):
+        by = scale_of(queries[:, :width].astype(jnp.float32))
+        for group in range(GROUPS):
+            for part in range(OWN):
+                at = lanes(group * OWN + part)
+                query = (queries[:, at].astype(jnp.float32) * by * gain[:, at]).astype(jnp.bfloat16)
+                if part < SLOTS:
+                    out[part * GROUPS + group, 0:ROWS, :] = query
+                    out[part * GROUPS + group, 2 * ROWS : Q_ROWS, :] = info
+                else:
+                    for slot in range(SLOTS):
+                        out[slot * GROUPS + group, ROWS : 2 * ROWS, :] = query
+
+    @pl.when(last)
+    def _():
+        spread(climbed, climbed[0:16, width:])
+
+    @pl.when(jnp.logical_not(last))
+    def _():
+        spread(own, jnp.full((16, HD), levels[0], jnp.int32).astype(jnp.float32).astype(jnp.bfloat16))
 
 
 def attend_kernel(
-    frames, first_out, planes, tile, offsets, mine, right, queries, gates, left_in, out_ref, key_all, value_all, key_part, value_part, out, sems, left, left_sem
+    frames, spans, places, copied, planes, tile, offsets, mine, queries, gates, *refs
 ):
+    edges, refs = refs[: len(spans)], refs[len(spans) :]
+    earlier, refs = refs[: len(places) - 1], refs[len(places) - 1 :]
+    out_ref, key_all, value_all, key_part, value_part, out, sems, done_sems, edge_sem, *room = refs
+    reads = []
+    if copied:
+        reads.append(pltpu.make_async_copy(edges[0], room[0], edge_sem.at[0]))
+        reads[0].start()
+        edges = (room[0], *edges[1:])
     plane = lax.axis_index("plane")
     slot = lax.axis_index("slot")
     count = planes * SLOTS
     phase = lax.rem(offsets[0] + W * count - (plane * SLOTS + slot), W)
     ones = jnp.ones((ROWS * GROUPS, HD), jnp.bfloat16)
-    below = None
-    if left_in is not None:
-        below = pltpu.make_async_copy(left_in, left, left_sem.at[0])
-        below.start()
+    writes = []
+    for n, (done, place) in enumerate(zip(earlier, places[1:])):
+        write = pltpu.make_async_copy(
+            done, out_ref.at[pl.ds(place * GROUPS, done.shape[0])], done_sems.at[n]
+        )
+        write.start()
+        writes.append(write)
     unpacked = set()
 
     def unpack(j):
         if j in unpacked:
             return
         unpacked.add(j)
-        if j < REACH:
-            if not waited:
-                below.wait()
-                waited.append(True)
-            ref, base = left, j * GROUPS
-        elif j < REACH + SLOTS:
-            ref, base = mine, (j - REACH) * GROUPS
+        if BELOW <= j < BELOW + SLOTS:
+            ref, base = mine, (j - BELOW) * GROUPS
         else:
-            ref, base = right, (j - REACH - SLOTS) * GROUPS
+            n = next(
+                n for n, span in enumerate(spans) if span <= j < span + edges[n].shape[0] // GROUPS
+            )
+            ref, base = edges[n], (j - spans[n]) * GROUPS
+            if n == 0 and reads:
+                reads.pop().wait()
         from_all = slice(base, base + GROUPS)
         key_all[j] = ref[from_all, 0:ROWS, :].reshape(ROWS * GROUPS, HD)
         key_part[j] = ref[from_all, ROWS : ROWS + PART, :].reshape(PART * GROUPS, HD)
@@ -117,8 +140,6 @@
         value_all[j, :, HD:] = ones
         value_part[j, :, 0:HD] = ref[from_all, 2 * ROWS + PART : KV_ROWS, :].reshape(PART * GROUPS, HD)
         value_part[j, :, HD:] = ones[: PART * GROUPS]
-
-    waited = []
 
     def softmaxed(query, key_ref, value_ref, start, allowed):
         scores = [
@@ -153,17 +174,20 @@
         jnp.int32, (ROWS * GROUPS, HD), 1
     )
     blocks_of = tile // ROWS
-    writes = []
     for i in reversed(frames):
-        for j in range(i + 2 * REACH, i - 1, -1):
+        for j in sorted(
+            range(i + BELOW - W + 1, i + BELOW + W),
+            key=lambda j: (copied and spans[0] <= j < spans[0] + edges[0].shape[0] // GROUPS, -j),
+        ):
             unpack(j)
         frame = plane * SLOTS + i
-        offset = lax.rem(frame + phase, W)
-        start = i + REACH - offset
+        offset = lax.rem(frame + W + phase, W)
+        start = i + BELOW - offset
         allowed = [
-            (frame - offset + b >= 0) & (frame - offset + b < count) for b in range(W)
+            (frame < 0) | (frame - offset + b >= 0) & (frame - offset + b < count) for b in range(W)
         ]
-        level = queries[i * GROUPS, 2 * ROWS : 2 * ROWS + 1, :].astype(jnp.float32)
+        at_slot = i % SLOTS
+        level = queries[at_slot * GROUPS, 2 * ROWS : 2 * ROWS + 1, :].astype(jnp.float32)
         picked = level_row == level
 
         def gate_of(at):
@@ -174,14 +198,14 @@
         to = (i - frames[0]) * GROUPS
 
         for n in range(ROWS * GROUPS // tile):
-            first = i * GROUPS + n * blocks_of
+            first = at_slot * GROUPS + n * blocks_of
             query = queries[first : first + blocks_of, 0:ROWS, :].reshape(tile, HD)
             _, numer, total = softmaxed(query, key_all, value_all, start, allowed)
             done = (numer / total * gate).astype(jnp.bfloat16).reshape(blocks_of, ROWS, HD)
             first = to + n * blocks_of
             out[first : first + blocks_of, 0:ROWS, :] = done
 
-        query = queries[i * GROUPS : (i + 1) * GROUPS, ROWS : 2 * ROWS, :].reshape(ROWS * GROUPS, HD)
+        query = queries[at_slot * GROUPS : (at_slot + 1) * GROUPS, ROWS : 2 * ROWS, :].reshape(ROWS * GROUPS, HD)
         top, numer, total = softmaxed(query, key_part, value_part, start, allowed)
         done = (numer / total * gate_shared).astype(jnp.bfloat16).reshape(GROUPS, ROWS, HD)
         out[to : to + GROUPS, ROWS : 2 * ROWS, :] = done
@@ -197,7 +221,7 @@
             out[to + t, 2 * ROWS : O_ROWS, :] = three.astype(jnp.bfloat16)
         write = pltpu.make_async_copy(
             out.at[pl.ds(to, GROUPS)],
-            out_ref.at[pl.ds(to + first_out * GROUPS, GROUPS)],
+            out_ref.at[pl.ds(places[0] * GROUPS + to, GROUPS)],
             sems.at[i - frames[0]],
         )
         write.start()
@@ -206,7 +230,7 @@
         write.wait()
 
 
-def combine_kernel(parts, residual, incoming, out_ref, out, sems):
+def combine_kernel(parts, residual_in, incoming, out_ref, residual, out, sems, in_sems):
     first = (lax.axis_index("plane") == 0) & (lax.axis_index("slot") == 0)
 
     @pl.when(first)
@@ -217,6 +241,11 @@
 
     @pl.when(jnp.logical_not(first))
     def _():
+        reads = []
+        for n in range(GROUPS // 2):
+            at = pl.ds(n * 2 * OWN * HD, 2 * OWN * HD)
+            reads.append(pltpu.make_async_copy(residual_in.at[:, at], residual.at[:, at], in_sems.at[n]))
+            reads[n].start()
         sent = parts[:, 2 * ROWS : O_ROWS, :].astype(jnp.float32)
         row = lax.broadcasted_iota(jnp.int32, sent.shape, 1)
         weight = jnp.sum(jnp.where(row < 3, sent, 0.0), axis=1).reshape(SLOTS, GROUPS, HD)
@@ -227,6 +256,8 @@
         weight = weight.T[:ROWS]
         writes = []
         for group in range(GROUPS):
+            if group % 2 == 0:
+                reads[group // 2].wait()
             shared = None
             for slot in range(SLOTS):
                 r = slot * GROUPS + group
@@ -259,7 +290,6 @@
     exchange = lambda x: lax.all_to_all(x, ("slot", "group"), 0, 0, tiled=True)
     up = [(z, z + 1) for z in range(planes - 1)]
     down = [(z + 1, z) for z in range(planes - 1)]
-    count = planes * SLOTS
 
     kv = pl.pallas_call(
         pack_kv_kernel,
@@ -278,40 +308,42 @@
         name="pack_kv",
     )(keys[0], values[0], k_gain[None])
     kv = exchange(kv)
-    climbed = lax.ppermute(
-        residual[0],
-        ("plane", "slot"),
-        [(z * SLOTS + SLOTS - 1, (z + 1) * SLOTS + SLOTS - 1) for z in range(planes - 1)],
+    last = SLOTS - 1
+    climb = [(z * SLOTS + last, (z + 1) * SLOTS + last) for z in range(planes - 1)]
+    level = jnp.broadcast_to(levels.astype(jnp.bfloat16), (ROWS, HD))
+    climbed_queries, climbed = (
+        lax.ppermute(x, ("plane", "slot"), climb)
+        for x in (jnp.concatenate([queries[0], level], axis=1), residual[0])
     )
-    queries, climbed = lax.optimization_barrier((queries, climbed))
     packed = pl.pallas_call(
         pack_q_kernel,
         out_shape=jax.ShapeDtypeStruct((dests, Q_ROWS, HD), jnp.bfloat16),
-        in_specs=[smem] + whole(2),
+        in_specs=[smem] + whole(3),
         out_specs=whole(1)[0],
         compiler_params=params(),
         name="pack_q",
-    )(levels, queries[0], q_gain[None])
+    )(levels, queries[0], climbed_queries, q_gain[None])
+    kv, climbed = lax.optimization_barrier((kv, climbed))
     query = exchange(packed)
-    shifted = jnp.where(lax.axis_index("slot") == SLOTS - 1, climbed, residual[0])
-    query, shifted = lax.optimization_barrier((query, shifted))
-    moved = lax.ppermute(shifted, "slot", [(i, (i + 1) % SLOTS) for i in range(SLOTS)])
-    edge = REACH * GROUPS
-    right = lax.ppermute(kv[:edge], "plane", down)
-    left = lax.ppermute(kv[dests - edge :], "plane", up)
-    def attend(frames, first_out, slots_out, name):
-        blocks = 2 * REACH + SLOTS
+    near = lax.ppermute(kv[2 * GROUPS :], "plane", up)
+    right = lax.ppermute(kv[:GROUPS], "plane", down)
+    far = lax.ppermute(kv[GROUPS : 2 * GROUPS], "plane", up)
+
+    def attend(frames, edges, place, earlier, slots_out, name, copied=True):
+        blocks = BELOW + SLOTS + ABOVE
         units = len(frames)
-        below = [left] if min(frames) < REACH else []
-
-        def kernel(*refs):
-            fixed, rest = refs[:5], refs[5:]
-            attend_kernel(frames, first_out, planes, 256, *fixed, *(rest if below else (None, *rest)))
-
         return pl.pallas_call(
-            kernel,
+            functools.partial(
+                attend_kernel,
+                frames,
+                [span for span, _ in edges],
+                [place] + [at for at, _ in earlier],
+                copied,
+                planes,
+                256,
+            ),
             out_shape=jax.ShapeDtypeStruct((slots_out * GROUPS, O_ROWS, HD), jnp.bfloat16),
-            in_specs=[smem] + whole(4) + [HBM] * len(below),
+            in_specs=[smem] + whole(3) + [HBM] * copied + whole(len(edges) - copied + len(earlier)),
             out_specs=HBM,
             scratch_shapes=[
                 VMEM((blocks, ROWS * GROUPS, HD), jnp.bfloat16),
@@ -320,28 +352,39 @@
                 VMEM((blocks, PART * GROUPS, 2 * HD), jnp.bfloat16),
                 VMEM((units * GROUPS, O_ROWS, HD), jnp.bfloat16),
                 pltpu.SemaphoreType.DMA((units,)),
-                VMEM((edge, KV_ROWS, HD), jnp.bfloat16),
+                pltpu.SemaphoreType.DMA((2,)),
                 pltpu.SemaphoreType.DMA((1,)),
-            ],
+            ]
+            + [VMEM(edges[0][1].shape, jnp.bfloat16)] * copied,
             compiler_params=params(32),
             cost_estimate=pl.CostEstimate(
                 flops=units * 500_000_000, bytes_accessed=4_000_000, transcendentals=units * 1_000_000
             ),
             name=name,
-        )(offsets, kv, right, query, gate_table, *below)
-
-    last = attend((SLOTS - 1,), 0, 1, "attend_last")
-    last = lax.ppermute(last, "plane", up)
-    others = attend(tuple(range(SLOTS - 1)), 1, SLOTS, "attend_others")
-    others, moved = lax.optimization_barrier((others, moved))
-    parts = exchange(lax.dynamic_update_slice(others, last, (0, 0, 0)))
+        )(offsets, kv, query, gate_table, *(x for _, x in edges), *(x for _, x in earlier))
+
+    shifted = jnp.where(lax.axis_index("slot") == last, climbed, residual[0])
+    moved = lax.ppermute(shifted, "slot", [(i, (i + 1) % SLOTS) for i in range(SLOTS)])
+    inner = attend((0, 1), [(1, near)], 0, [], 2, "attend_inner", False)
+    inner, query = lax.optimization_barrier((inner, query))
+    upper = attend((2,), [(BELOW + SLOTS, right)], 0, [], 1, "attend_upper")
+    upper, query = lax.optimization_barrier((upper, query))
+    attended = attend((-1,), [(0, far), (1, near)], 0, [(1, inner), (3, upper)], SLOTS, "attend_lower")
+    attended, moved = lax.optimization_barrier((attended, moved))
+    parts = exchange(attended)
     updated = pl.pallas_call(
         combine_kernel,
         out_shape=jax.ShapeDtypeStruct(incoming.shape, jnp.bfloat16),
-        in_specs=whole(3),
+        in_specs=[pl.BlockSpec(memory_space=VMEM), HBM, pl.BlockSpec(memory_space=VMEM)],
         out_specs=HBM,
-        scratch_shapes=[VMEM(incoming.shape, jnp.bfloat16), pltpu.SemaphoreType.DMA((GROUPS // 2,))],
-        compiler_params=params(),
+        scratch_shapes=[
+            VMEM(incoming.shape, jnp.bfloat16),
+            VMEM(incoming.shape, jnp.bfloat16),
+            pltpu.SemaphoreType.DMA((GROUPS // 2,)),
+            pltpu.SemaphoreType.DMA((GROUPS // 2,)),
+        ],
+        compiler_params=params(20),
+        cost_estimate=pl.CostEstimate(flops=1_000, bytes_accessed=4_000_000, transcendentals=0),
         name="combine",
     )(parts, moved, incoming)
     return updated[None]

time: 97.8 us -> 96.8 us (0.990)
  waiting for transfers between devices: 28.4 us -> 19 us
  starting transfers between devices: 25.2 us -> 28.6 us
  local copies, waits for them, and re-layouts: 1.23 us -> 2.86 us
  Pallas kernels: 14.1 us -> 15.7 us
  other arithmetic: 0.91 us -> 2.01 us
    all_to_all x2, waiting for transfers between devices: 28.3 us -> 19 us  [on_device(): exchange = lambda x: lax.all_to_all(x, ('slot', 'group'), 0, 0, tiled=True)]
    ppermute x1, starting transfers between devices: 1.91 us -> 3.81 us  [on_device(): lax.ppermute(shifted, 'slot', [(i, (i + 1) % SLOTS) for i in range(SLOTS)])]
    pallas_call x2 -> x3, Pallas kernels: 8.26 us -> 9.91 us  [attend(): pl.pallas_call(functools.partial(attend_kernel, frames, [span for span, _...]
    ppermute x4 -> x5, starting transfers between devices: 8.64 us -> 10.2 us  [the longest x1 4.87 us: on_device(): far = lax.ppermute(kv[GROUPS:2 * GROUPS], 'plane', up)]
    select_n x1, other arithmetic: 0.91 us -> 2.01 us  [on_device(): shifted = jnp.where(lax.axis_index('slot') == last, climbed, residual[0])]
    pallas_call x1, Pallas kernels: 1.33 us -> 0.32 us  [on_device(): pl.pallas_call(pack_q_kernel, out_shape=jax.ShapeDtypeStruct((dests, Q_RO...]
    unnamed x16 -> x10, local copies, waits for them, and re-layouts: 0.04 us -> 1.03 us
  transfers between devices with their start and end apart: 7 -> 8, of which waited for: 2 -> 2; matrix products, arithmetic and copies ran while one was open for 2% -> 4% of each run, Pallas kernels for 10% -> 11%
where the time goes in v3:
time: 96.8 us; the launch traced here: 95.2 us
  starting transfers between devices  28.6 us (30%)
  blocking collectives  25.5 us (26%)
  waiting for transfers between devices  19 us (20%)
  Pallas kernels  15.7 us (16%)
  local copies, waits for them, and re-layouts  2.86 us (3%)
  other arithmetic  2.01 us (2%)
  between operations  1.49 us (2%)
    all_to_all x1, blocking collectives, on_device(): exchange = lambda x: lax.all_to_all(x, ('slot', 'group'), 0, 0, tiled=True)  25.5 us
    all_to_all x2, waiting for transfers between devices, on_device(): exchange = lambda x: lax.all_to_all(x, ('slot', 'group'), 0, 0, tiled=True)  19 us
    all_to_all x2, starting transfers between devices, on_device(): exchange = lambda x: lax.all_to_all(x, ('slot', 'group'), 0, 0, tiled=True)  14.6 us
    pallas_call x3, Pallas kernels, attend(): pl.pallas_call(functools.partial(attend_kernel, frames, [span for span, _...  9.91 us
    ppermute x1, starting transfers between devices, on_device(): far = lax.ppermute(kv[GROUPS:2 * GROUPS], 'plane', up)  4.87 us
    ppermute x1, starting transfers between devices, on_device(): lax.ppermute(shifted, 'slot', [(i, (i + 1) % SLOTS) for i in range(SLOTS)])  3.81 us
    pallas_call x1, Pallas kernels, on_device(): pl.pallas_call(pack_kv_kernel, out_shape=jax.ShapeDtypeStruct((dests, KV_...  3.25 us
    pallas_call x1, Pallas kernels, on_device(): pl.pallas_call(combine_kernel, out_shape=jax.ShapeDtypeStruct(incoming.sh...  2.26 us
  transfers between devices with their start and end apart: 8, of which 2 were waited for; matrix products, arithmetic and copies ran while one was open for 4% of the time, Pallas kernels for 11%

profile of v3, /device:TPU:1, one launch (start us, length us, event | category | flops | bytes accessed | tf_op | source)
XLA Modules:
  0.0 95.2 jit_solution(9024257900431255662)
XLA Ops:
  0.0 3.3 %pack_kv.1 = bf16[32,160,128]{2,1,0:T(8,128)(2,1)} custom-call(bf16[64,5120]{1,0:T(8,128)(2,1)} %bitcast.12, bf16[64,5120]{1,0:T(8,128)(2,1)} %bitcast.13, f32[1,5120]{1,0:T(1,128)} %bitcast.14), custom_call_target="tpu_custom_call" | custom-call | flops 1000000 | bytes 40000000 | tf_op jit(solution)/shard_map/pack_kv/pallas_call | solution.py:294
  3.3 0.0 copy-start.2
  3.3 10.7 %all-to-all-start = ((bf16[32,160,128]{2,1,0:T(8,128)(2,1)}), bf16[32,160,128]{2,1,0:T(8,128)(2,1)S(1)}, u32[]{:S(2)}, u32[]{:S(2)}) async-start(bf16[32,160,128]{2,1,0:T(8,128)(2,1)} %pack_kv.1), calls=%async_computation | async-start | bytes 2621440 | tf_op jit(solution)/shard_map/all_to_all | solution.py:290
  14.0 0.0 copy-start.4
  14.6 0.0 copy-done.2
  14.7 0.7 collective-permute-start.1
  15.4 1.5 %collective-permute-start = (bf16[64,5120]{1,0:T(8,128)(2,1)}, bf16[64,5120]{1,0:T(8,128)(2,1)}, u32[]{:S(2)}, u32[]{:S(2)}) collective-permute-start(bf16[64,5120]{1,0:T(8,128)(2,1)} %bitcast.3), channel_id=1, source_target_pairs={{24,56},{56,88},{88,120},{120,152},{152,184},{184,216},{216,248},{... | collective-permute-start | bytes 1966088 | tf_op jit(solution)/shard_map/ppermute | solution.py:315
  16.9 0.0 collective-permute-done.1.climbed
  16.9 0.0 copy-done.4
  16.9 0.3 pack_q.1
  17.3 1.0 %copy-done = bf16[32,144,128]{2,1,0:T(8,128)(2,1)} copy-done((bf16[32,144,128]{2,1,0:T(8,128)(2,1)}, bf16[32,144,128]{2,1,0:T(8,128)(2,1)S(1)}, u32[]{:S(2)}) %copy-start) | copy-done | bytes 1179672
  18.3 16.1 %all-to-all-done.mine = bf16[32,160,128]{2,1,0:T(8,128)(2,1)S(1)} async-done(((bf16[32,160,128]{2,1,0:T(8,128)(2,1)}), bf16[32,160,128]{2,1,0:T(8,128)(2,1)S(1)}, u32[]{:S(2)}, u32[]{:S(2)}) %all-to-all-start) | async-done | bytes 1310752 | tf_op jit(solution)/shard_map/all_to_all | solution.py:290
  34.4 4.0 %all-to-all-start.1 = ((bf16[32,144,128]{2,1,0:T(8,128)(2,1)}), bf16[32,144,128]{2,1,0:T(8,128)(2,1)S(1)}, u32[]{:S(2)}, u32[]{:S(2)}) async-start(bf16[32,144,128]{2,1,0:T(8,128)(2,1)} %copy-done), calls=%async_computation.1 | async-start | bytes 2359296 | tf_op jit(solution)/shard_map/all_to_all | solution.py:290
  38.4 0.0 collective-permute-done
  38.4 0.9 slice.9
  39.3 1.8 %collective-permute-start.2 = (bf16[16,160,128]{2,1,0:T(8,128)(2,1)}, bf16[16,160,128]{2,1,0:T(8,128)(2,1)S(1)}, u32[]{:S(2)}, u32[]{:S(2)}) collective-permute-start(bf16[16,160,128]{2,1,0:T(8,128)(2,1)} %slice.9), channel_id=1, source_target_pairs={{0,32},{32,64},{64,96},{96,128},{128,160},{160,192},{192,224},{224... | collective-permute-start | bytes 1966088 | tf_op jit(solution)/shard_map/ppermute | solution.py:328
  41.1 2.0 %broadcast_select_fusion = bf16[64,5120]{1,0:T(8,128)(2,1)} fusion(bf16[64,5120]{1,0:T(8,128)(2,1)} %collective-permute-done, pred[]{:T(512)S(6)} %eq.3, bf16[1,64,5120]{2,1,0:T(8,128)(2,1)} %param.13), kind=kLoop, calls=%fused_computation | loop fusion | flops 327680 | bytes 1966081 | tf_op jit(solution)/shard_map/jit(_where)/select_n | solution.py:366
  43.1 3.8 %collective-permute-start.5 = (bf16[64,5120]{1,0:T(8,128)(2,1)}, bf16[64,5120]{1,0:T(8,128)(2,1)}, u32[]{:S(2)}, u32[]{:S(2)}) collective-permute-start(bf16[64,5120]{1,0:T(8,128)(2,1)} %broadcast_select_fusion), channel_id=1, source_target_pairs={{0,8},{8,16},{16,24},{24,0},{1,9},{9,17},{17,25},{25,1},{2,10},{10... | collective-permute-start | bytes 1966088 | tf_op jit(solution)/shard_map/ppermute | solution.py:367
  46.9 0.9 fusion
  47.8 1.3 %collective-permute-start.3 = (bf16[8,160,128]{2,1,0:T(8,128)(2,1)}, bf16[8,160,128]{2,1,0:T(8,128)(2,1)}, u32[]{:S(2)}, u32[]{:S(2)}) collective-permute-start(bf16[8,160,128]{2,1,0:T(8,128)(2,1)} %get-tuple-element.22), channel_id=1, source_target_pairs={{32,0},{64,32},{96,64},{128,96},{160,128},{192,160},{224,192},{256... | collective-permute-start | bytes 983048 | tf_op jit(solution)/shard_map/ppermute | solution.py:329
  49.1 4.9 %collective-permute-start.4 = (bf16[8,160,128]{2,1,0:T(8,128)(2,1)}, bf16[8,160,128]{2,1,0:T(8,128)(2,1)}, u32[]{:S(2)}, u32[]{:S(2)}) collective-permute-start(bf16[8,160,128]{2,1,0:T(8,128)(2,1)} %get-tuple-element.21), channel_id=1, source_target_pairs={{0,32},{32,64},{64,96},{96,128},{128,160},{160,192},{192,224},{224... | collective-permute-start | bytes 983048 | tf_op jit(solution)/shard_map/ppermute | solution.py:330
  54.6 2.9 %all-to-all-done.1.queries = bf16[32,144,128]{2,1,0:T(8,128)(2,1)S(1)} async-done(((bf16[32,144,128]{2,1,0:T(8,128)(2,1)}), bf16[32,144,128]{2,1,0:T(8,128)(2,1)S(1)}, u32[]{:S(2)}, u32[]{:S(2)}) %all-to-all-start.1) | async-done | bytes 1179680 | tf_op jit(solution)/shard_map/all_to_all | solution.py:290
  57.5 0.0 collective-permute-done.2.refs_0_.refs_1_
  57.5 4.2 %attend_inner.1.refs_2_ = bf16[16,144,128]{2,1,0:T(8,128)(2,1)S(1)} custom-call(s32[1]{0:T(128)S(6)} %copy.12.offsets, bf16[32,160,128]{2,1,0:T(8,128)(2,1)S(1)} %all-to-all-done.mine, bf16[32,144,128]{2,1,0:T(8,128)(2,1)S(1)} %all-to-all-done.1.queries, f32[128,640]{1,0:T(8,128)S(1)} %copy-done.1, ...), custom_call_target="tpu_custom_call" | custom-call | flops 1000000000 | bytes 4000000 | tf_op jit(solution)/shard_map/attend_inner/pallas_call | solution.py:335
  61.7 0.0 collective-permute-done.3.refs_0_
  61.7 2.9 %attend_upper.1.refs_3_ = bf16[8,144,128]{2,1,0:T(8,128)(2,1)S(1)} custom-call(s32[1]{0:T(128)S(6)} %copy.12.offsets, bf16[32,160,128]{2,1,0:T(8,128)(2,1)S(1)} %all-to-all-done.mine, bf16[32,144,128]{2,1,0:T(8,128)(2,1)S(1)} %all-to-all-done.1.queries, f32[128,640]{1,0:T(8,128)S(1)} %copy-done.1, bf16[8,160,128]{2,1,0:T(8,128)(2,1)} %collective-permute-done.3.refs_0_), custom_call_target="tpu_custom_call" | custom-call | flops 500000000 | bytes 4000000 | tf_op jit(solution)/shard_map/attend_upper/pallas_call | solution.py:335
  64.6 0.0 collective-permute-done.4.refs_0_
  64.6 2.9 %attend_lower.1 = bf16[32,144,128]{2,1,0:T(8,128)(2,1)S(1)} custom-call(s32[1]{0:T(128)S(6)} %copy.12.offsets, bf16[32,160,128]{2,1,0:T(8,128)(2,1)S(1)} %all-to-all-done.mine, bf16[32,144,128]{2,1,0:T(8,128)(2,1)S(1)} %all-to-all-done.1.queries, f32[128,640]{1,0:T(8,128)S(1)} %copy-done.1, bf16[8,160,128]{2,1,0:T(8,128)(2,1)} %collective-permute-done.4.refs_0_, ...), custom_call_target="tpu_custom_call" | custom-call | flops 500000000 | bytes 4000000 | tf_op jit(solution)/shard_map/attend_lower/pallas_call | solution.py:335
  67.4 0.0 copy-start.3
  67.5 0.0 collective-permute-done.5.residual_in
  67.5 25.5 %all_to_all.15.parts = bf16[32,144,128]{2,1,0:T(8,128)(2,1)S(1)} all-to-all(bf16[32,144,128]{2,1,0:T(8,128)(2,1)S(1)} %attend_lower.1), channel_id=1, replica_groups=mesh['plane'=16,'slot'=4,'group'=8] {'slot','group'}, dimensions={0} | all-to-all | bytes 2359296 | tf_op jit(solution)/shard_map/all_to_all | solution.py:290
  93.0 2.3 %combine.1 = bf16[64,5120]{1,0:T(8,128)(2,1)} custom-call(bf16[32,144,128]{2,1,0:T(8,128)(2,1)S(1)} %all_to_all.15.parts, bf16[64,5120]{1,0:T(8,128)(2,1)} %collective-permute-done.5.residual_in, bf16[64,5120]{1,0:T(8,128)(2,1)S(1)} %copy-done.3), custom_call_target="tpu_custom_call" | custom-call | flops 1000 | bytes 4000000 | tf_op jit(solution)/shard_map/combine/pallas_call | solution.py:375
  (5 shorter events, 0.1 us)
Async XLA Ops:
  3.3 11.4 %copy-start.2 = (bf16[1,64,5120]{2,1,0:T(8,128)(2,1)S(1)}, bf16[1,64,5120]{2,1,0:T(8,128)(2,1)}, u32[]{:S(2)}) copy-start(bf16[1,64,5120]{2,1,0:T(8,128)(2,1)} %param.10) | copy-start | bytes 1966084
  3.3 31.1 %all-to-all-start = ((bf16[32,160,128]{2,1,0:T(8,128)(2,1)}), bf16[32,160,128]{2,1,0:T(8,128)(2,1)S(1)}, u32[]{:S(2)}, u32[]{:S(2)}) async-start(bf16[32,160,128]{2,1,0:T(8,128)(2,1)} %pack_kv.1), calls=%async_computation | async-start | bytes 2621440 | tf_op jit(solution)/shard_map/all_to_all | solution.py:290
  14.0 3.0 %copy-start.4 = (f32[5120]{0:T(1024)S(1)}, f32[5120]{0:T(1024)}, u32[]{:S(2)}) copy-start(f32[5120]{0:T(1024)} %param.14) | copy-start | bytes 61444
  14.7 2.2 %collective-permute-start.1 = (bf16[64,5248]{1,0:T(8,128)(2,1)S(1)}, bf16[64,5248]{1,0:T(8,128)(2,1)S(1)}, u32[]{:S(2)}, u32[]{:S(2)}) collective-permute-start(bf16[64,5248]{1,0:T(8,128)(2,1)S(1)} %concatenate.3), channel_id=1, source_target_pairs={{24,56},{56,88},{88,120},{120,152},{152,184},{184,216},{216,248},{... | collective-permute-start | bytes 2015240 | tf_op jit(solution)/shard_map/ppermute | solution.py:315
  15.4 23.0 %collective-permute-start = (bf16[64,5120]{1,0:T(8,128)(2,1)}, bf16[64,5120]{1,0:T(8,128)(2,1)}, u32[]{:S(2)}, u32[]{:S(2)}) collective-permute-start(bf16[64,5120]{1,0:T(8,128)(2,1)} %bitcast.3), channel_id=1, source_target_pairs={{24,56},{56,88},{88,120},{120,152},{152,184},{184,216},{216,248},{... | collective-permute-start | bytes 1966088 | tf_op jit(solution)/shard_map/ppermute | solution.py:315
  17.3 1.0 %copy-start = (bf16[32,144,128]{2,1,0:T(8,128)(2,1)}, bf16[32,144,128]{2,1,0:T(8,128)(2,1)S(1)}, u32[]{:S(2)}) copy-start(bf16[32,144,128]{2,1,0:T(8,128)(2,1)S(1)} %pack_q.1) | copy-start | bytes 3538948
  34.4 23.1 %all-to-all-start.1 = ((bf16[32,144,128]{2,1,0:T(8,128)(2,1)}), bf16[32,144,128]{2,1,0:T(8,128)(2,1)S(1)}, u32[]{:S(2)}, u32[]{:S(2)}) async-start(bf16[32,144,128]{2,1,0:T(8,128)(2,1)} %copy-done), calls=%async_computation.1 | async-start | bytes 2359296 | tf_op jit(solution)/shard_map/all_to_all | solution.py:290
  39.3 18.2 %copy-start.1 = (f32[128,640]{1,0:T(8,128)S(1)}, f32[128,640]{1,0:T(8,128)}, u32[]{:S(2)}) copy-start(f32[128,640]{1,0:T(8,128)} %gates.5) | copy-start | bytes 983044
  39.3 18.2 %collective-permute-start.2 = (bf16[16,160,128]{2,1,0:T(8,128)(2,1)}, bf16[16,160,128]{2,1,0:T(8,128)(2,1)S(1)}, u32[]{:S(2)}, u32[]{:S(2)}) collective-permute-start(bf16[16,160,128]{2,1,0:T(8,128)(2,1)} %slice.9), channel_id=1, source_target_pairs={{0,32},{32,64},{64,96},{96,128},{128,160},{160,192},{192,224},{224... | collective-permute-start | bytes 1966088 | tf_op jit(solution)/shard_map/ppermute | solution.py:328
  43.1 24.4 %collective-permute-start.5 = (bf16[64,5120]{1,0:T(8,128)(2,1)}, bf16[64,5120]{1,0:T(8,128)(2,1)}, u32[]{:S(2)}, u32[]{:S(2)}) collective-permute-start(bf16[64,5120]{1,0:T(8,128)(2,1)} %broadcast_select_fusion), channel_id=1, source_target_pairs={{0,8},{8,16},{16,24},{24,0},{1,9},{9,17},{17,25},{25,1},{2,10},{10... | collective-permute-start | bytes 1966088 | tf_op jit(solution)/shard_map/ppermute | solution.py:367
  47.8 13.9 %collective-permute-start.3 = (bf16[8,160,128]{2,1,0:T(8,128)(2,1)}, bf16[8,160,128]{2,1,0:T(8,128)(2,1)}, u32[]{:S(2)}, u32[]{:S(2)}) collective-permute-start(bf16[8,160,128]{2,1,0:T(8,128)(2,1)} %get-tuple-element.22), channel_id=1, source_target_pairs={{32,0},{64,32},{96,64},{128,96},{160,128},{192,160},{224,192},{256... | collective-permute-start | bytes 983048 | tf_op jit(solution)/shard_map/ppermute | solution.py:329
  49.1 15.5 %collective-permute-start.4 = (bf16[8,160,128]{2,1,0:T(8,128)(2,1)}, bf16[8,160,128]{2,1,0:T(8,128)(2,1)}, u32[]{:S(2)}, u32[]{:S(2)}) collective-permute-start(bf16[8,160,128]{2,1,0:T(8,128)(2,1)} %get-tuple-element.21), channel_id=1, source_target_pairs={{0,32},{32,64},{64,96},{96,128},{128,160},{160,192},{192,224},{224... | collective-permute-start | bytes 983048 | tf_op jit(solution)/shard_map/ppermute | solution.py:330
  67.4 25.5 %copy-start.3 = (bf16[64,5120]{1,0:T(8,128)(2,1)S(1)}, bf16[64,5120]{1,0:T(8,128)(2,1)}, u32[]{:S(2)}) copy-start(bf16[64,5120]{1,0:T(8,128)(2,1)} %incoming.1) | copy-start | bytes 1966084

commit v4 on v3

--- a/solution.py
+++ b/solution.py
@@ -174,7 +174,7 @@
         jnp.int32, (ROWS * GROUPS, HD), 1
     )
     blocks_of = tile // ROWS
-    for i in reversed(frames):
+    for i in sorted(frames, key=lambda i: (i == SLOTS - 2, -i)):
         for j in sorted(
             range(i + BELOW - W + 1, i + BELOW + W),
             key=lambda j: (copied and spans[0] <= j < spans[0] + edges[0].shape[0] // GROUPS, -j),
@@ -365,11 +365,9 @@
 
     shifted = jnp.where(lax.axis_index("slot") == last, climbed, residual[0])
     moved = lax.ppermute(shifted, "slot", [(i, (i + 1) % SLOTS) for i in range(SLOTS)])
-    inner = attend((0, 1), [(1, near)], 0, [], 2, "attend_inner", False)
-    inner, query = lax.optimization_barrier((inner, query))
-    upper = attend((2,), [(BELOW + SLOTS, right)], 0, [], 1, "attend_upper")
+    upper = attend((0, 1, 2), [(BELOW + SLOTS, right), (1, near)], 0, [], 3, "attend_upper")
     upper, query = lax.optimization_barrier((upper, query))
-    attended = attend((-1,), [(0, far), (1, near)], 0, [(1, inner), (3, upper)], SLOTS, "attend_lower")
+    attended = attend((-1,), [(0, far), (1, near)], 0, [(1, upper)], SLOTS, "attend_lower")
     attended, moved = lax.optimization_barrier((attended, moved))
     parts = exchange(attended)
     updated = pl.pallas_call(

time: 96.8 us -> 100 us (1.033)
  the two profiles are of different devices: /device:TPU:1 before, /device:TPU:97 now
where the time goes in v4:
time: 100 us; the launch traced here: 99.3 us
  starting transfers between devices  29.3 us (29%)
  blocking collectives  26.4 us (26%)
  waiting for transfers between devices  20.6 us (21%)
  Pallas kernels  16 us (16%)
  local copies, waits for them, and re-layouts  3.42 us (3%)
  other arithmetic  2.02 us (2%)
  between operations  1.48 us (1%)
    all_to_all x1, blocking collectives, on_device(): exchange = lambda x: lax.all_to_all(x, ('slot', 'group'), 0, 0, tiled=True)  26.4 us
    all_to_all x2, waiting for transfers between devices, on_device(): exchange = lambda x: lax.all_to_all(x, ('slot', 'group'), 0, 0, tiled=True)  16.1 us
    all_to_all x2, starting transfers between devices, on_device(): exchange = lambda x: lax.all_to_all(x, ('slot', 'group'), 0, 0, tiled=True)  11.9 us
    pallas_call x2, Pallas kernels, attend(): pl.pallas_call(functools.partial(attend_kernel, frames, [span for span, _...  9.24 us
    ppermute x1, starting transfers between devices, on_device(): near = lax.ppermute(kv[2 * GROUPS:], 'plane', up)  4.88 us
    ppermute x1, starting transfers between devices, on_device(): far = lax.ppermute(kv[GROUPS:2 * GROUPS], 'plane', up)  4.57 us
    ppermute x1, waiting for transfers between devices, on_device(): right = lax.ppermute(kv[:GROUPS], 'plane', down)  4.45 us
    ppermute x1, starting transfers between devices, on_device(): lax.ppermute(shifted, 'slot', [(i, (i + 1) % SLOTS) for i in range(SLOTS)])  3.81 us
  transfers between devices with their start and end apart: 8, of which 2 were waited for; matrix products, arithmetic and copies ran while one was open for 4% of the time, Pallas kernels for 11%

profile of v4, /device:TPU:97, one launch (start us, length us, event | category | flops | bytes accessed | tf_op | source)
XLA Modules:
  0.0 99.3 jit_solution(941173799657414276)
XLA Ops:
  0.0 3.2 %pack_kv.1 = bf16[32,160,128]{2,1,0:T(8,128)(2,1)} custom-call(bf16[64,5120]{1,0:T(8,128)(2,1)} %bitcast.12, bf16[64,5120]{1,0:T(8,128)(2,1)} %bitcast.13, f32[1,5120]{1,0:T(1,128)} %bitcast.14), custom_call_target="tpu_custom_call" | custom-call | flops 1000000 | bytes 40000000 | tf_op jit(solution)/shard_map/pack_kv/pallas_call | solution.py:294
  3.2 0.0 copy-start
  3.2 7.9 %all-to-all-start = ((bf16[32,160,128]{2,1,0:T(8,128)(2,1)}), bf16[32,160,128]{2,1,0:T(8,128)(2,1)S(1)}, u32[]{:S(2)}, u32[]{:S(2)}) async-start(bf16[32,160,128]{2,1,0:T(8,128)(2,1)} %pack_kv.1), calls=%async_computation | async-start | bytes 2621440 | tf_op jit(solution)/shard_map/all_to_all | solution.py:290
  11.1 0.0 copy-start.3
  11.8 0.0 copy-done
  11.9 0.7 collective-permute-start.1
  12.6 1.5 %collective-permute-start = (bf16[64,5120]{1,0:T(8,128)(2,1)}, bf16[64,5120]{1,0:T(8,128)(2,1)}, u32[]{:S(2)}, u32[]{:S(2)}) collective-permute-start(bf16[64,5120]{1,0:T(8,128)(2,1)} %bitcast.3), channel_id=1, source_target_pairs={{24,56},{56,88},{88,120},{120,152},{152,184},{184,216},{216,248},{... | collective-permute-start | bytes 1966088 | tf_op jit(solution)/shard_map/ppermute | solution.py:315
  14.1 0.0 collective-permute-done.1.climbed
  14.1 0.0 copy-done.3
  14.1 1.3 %pack_q.1 = bf16[32,144,128]{2,1,0:T(8,128)(2,1)} custom-call(s32[1]{0:T(128)S(6)} %copy.11.levels, bf16[64,5120]{1,0:T(8,128)(2,1)S(1)} %bitcast.10, bf16[64,5248]{1,0:T(8,128)(2,1)S(1)} %collective-permute-done.1.climbed, f32[1,5120]{1,0:T(1,128)S(1)} %bitcast.11), custom_call_target="tpu_custom_call" | custom-call | tf_op jit(solution)/shard_map/pack_q/pallas_call | solution.py:318
  15.5 16.1 %all-to-all-done.mine = bf16[32,160,128]{2,1,0:T(8,128)(2,1)S(1)} async-done(((bf16[32,160,128]{2,1,0:T(8,128)(2,1)}), bf16[32,160,128]{2,1,0:T(8,128)(2,1)S(1)}, u32[]{:S(2)}, u32[]{:S(2)}) %all-to-all-start) | async-done | bytes 1310752 | tf_op jit(solution)/shard_map/all_to_all | solution.py:290
  31.6 4.0 %all-to-all-start.1 = ((bf16[32,144,128]{2,1,0:T(8,128)(2,1)}), bf16[32,144,128]{2,1,0:T(8,128)(2,1)S(1)}, u32[]{:S(2)}, u32[]{:S(2)}) async-start(bf16[32,144,128]{2,1,0:T(8,128)(2,1)} %pack_q.1), calls=%async_computation.1 | async-start | bytes 2359296 | tf_op jit(solution)/shard_map/all_to_all | solution.py:290
  35.6 0.0 collective-permute-done
  35.6 0.9 slice.10
  36.5 4.9 %collective-permute-start.3 = (bf16[16,160,128]{2,1,0:T(8,128)(2,1)}, bf16[16,160,128]{2,1,0:T(8,128)(2,1)S(1)}, u32[]{:S(2)}, u32[]{:S(2)}) collective-permute-start(bf16[16,160,128]{2,1,0:T(8,128)(2,1)} %slice.10), channel_id=1, source_target_pairs={{0,32},{32,64},{64,96},{96,128},{128,160},{160,192},{192,224},{224... | collective-permute-start | bytes 1966088 | tf_op jit(solution)/shard_map/ppermute | solution.py:328
  41.4 2.0 %broadcast_select_fusion = bf16[64,5120]{1,0:T(8,128)(2,1)} fusion(bf16[64,5120]{1,0:T(8,128)(2,1)} %collective-permute-done, pred[]{:T(512)S(6)} %eq.3, bf16[1,64,5120]{2,1,0:T(8,128)(2,1)} %param.13), kind=kLoop, calls=%fused_computation | loop fusion | flops 327680 | bytes 1966081 | tf_op jit(solution)/shard_map/jit(_where)/select_n | solution.py:366
  43.4 3.8 %collective-permute-start.5 = (bf16[64,5120]{1,0:T(8,128)(2,1)}, bf16[64,5120]{1,0:T(8,128)(2,1)}, u32[]{:S(2)}, u32[]{:S(2)}) collective-permute-start(bf16[64,5120]{1,0:T(8,128)(2,1)} %broadcast_select_fusion), channel_id=1, source_target_pairs={{0,8},{8,16},{16,24},{24,0},{1,9},{9,17},{17,25},{25,1},{2,10},{10... | collective-permute-start | bytes 1966088 | tf_op jit(solution)/shard_map/ppermute | solution.py:367
  47.2 0.8 fusion
  48.0 1.9 %collective-permute-start.2 = (bf16[8,160,128]{2,1,0:T(8,128)(2,1)S(1)}, bf16[8,160,128]{2,1,0:T(8,128)(2,1)S(1)}, u32[]{:S(2)}, u32[]{:S(2)}) collective-permute-start(bf16[8,160,128]{2,1,0:T(8,128)(2,1)S(1)} %get-tuple-element.18), channel_id=1, source_target_pairs={{32,0},{64,32},{96,64},{128,96},{160,128},{192,160},{224,192},{256... | collective-permute-start | bytes 983048 | tf_op jit(solution)/shard_map/ppermute | solution.py:329
  49.9 4.6 %collective-permute-start.4 = (bf16[8,160,128]{2,1,0:T(8,128)(2,1)}, bf16[8,160,128]{2,1,0:T(8,128)(2,1)}, u32[]{:S(2)}, u32[]{:S(2)}) collective-permute-start(bf16[8,160,128]{2,1,0:T(8,128)(2,1)} %get-tuple-element.17), channel_id=1, source_target_pairs={{0,32},{32,64},{64,96},{96,128},{128,160},{160,192},{192,224},{224... | collective-permute-start | bytes 983048 | tf_op jit(solution)/shard_map/ppermute | solution.py:330
  55.1 4.5 %collective-permute-done.2.refs_0_ = bf16[8,160,128]{2,1,0:T(8,128)(2,1)S(1)} collective-permute-done((bf16[8,160,128]{2,1,0:T(8,128)(2,1)S(1)}, bf16[8,160,128]{2,1,0:T(8,128)(2,1)S(1)}, u32[]{:S(2)}, u32[]{:S(2)}) %collective-permute-start.2) | collective-permute-done | bytes 327712 | tf_op jit(solution)/shard_map/ppermute | solution.py:329
  59.6 0.7 copy-done.4
  60.3 0.0 all-to-all-done.1.queries
  60.3 0.0 collective-permute-done.3.refs_1_
  60.3 1.0 copy-done.5
  61.3 6.4 %attend_upper.1.refs_2_ = bf16[24,144,128]{2,1,0:T(8,128)(2,1)S(1)} custom-call(s32[1]{0:T(128)S(6)} %copy.12.offsets, bf16[32,160,128]{2,1,0:T(8,128)(2,1)S(1)} %all-to-all-done.mine, bf16[32,144,128]{2,1,0:T(8,128)(2,1)S(1)} %all-to-all-done.1.queries, f32[128,640]{1,0:T(8,128)S(1)} %copy-done.2, bf16[8,160,128]{2,1,0:T(8,128)(2,1)S(1)} %copy-done.5, ...), custom_call_target="tpu_custom_call" | custom-call | flops 1500000000 | bytes 4000000 | tf_op jit(solution)/shard_map/attend_upper/pallas_call | solution.py:335
  67.7 0.0 collective-permute-done.4.refs_0_
  67.7 2.9 %attend_lower.1 = bf16[32,144,128]{2,1,0:T(8,128)(2,1)S(1)} custom-call(s32[1]{0:T(128)S(6)} %copy.12.offsets, bf16[32,160,128]{2,1,0:T(8,128)(2,1)S(1)} %all-to-all-done.mine, bf16[32,144,128]{2,1,0:T(8,128)(2,1)S(1)} %all-to-all-done.1.queries, f32[128,640]{1,0:T(8,128)S(1)} %copy-done.2, bf16[8,160,128]{2,1,0:T(8,128)(2,1)} %collective-permute-done.4.refs_0_, ...), custom_call_target="tpu_custom_call" | custom-call | flops 500000000 | bytes 4000000 | tf_op jit(solution)/shard_map/attend_lower/pallas_call | solution.py:335
  70.6 0.0 copy-start.1
  70.6 0.0 collective-permute-done.5.residual_in
  70.6 26.4 %all_to_all.15.parts = bf16[32,144,128]{2,1,0:T(8,128)(2,1)S(1)} all-to-all(bf16[32,144,128]{2,1,0:T(8,128)(2,1)S(1)} %attend_lower.1), channel_id=1, replica_groups=mesh['plane'=16,'slot'=4,'group'=8] {'slot','group'}, dimensions={0} | all-to-all | bytes 2359296 | tf_op jit(solution)/shard_map/all_to_all | solution.py:290
  97.0 2.3 %combine.1 = bf16[64,5120]{1,0:T(8,128)(2,1)} custom-call(bf16[32,144,128]{2,1,0:T(8,128)(2,1)S(1)} %all_to_all.15.parts, bf16[64,5120]{1,0:T(8,128)(2,1)} %collective-permute-done.5.residual_in, bf16[64,5120]{1,0:T(8,128)(2,1)S(1)} %copy-done.1), custom_call_target="tpu_custom_call" | custom-call | flops 1000 | bytes 4000000 | tf_op jit(solution)/shard_map/combine/pallas_call | solution.py:373
  (6 shorter events, 0.1 us)
Async XLA Ops:
  3.2 8.6 %copy-start = (bf16[1,64,5120]{2,1,0:T(8,128)(2,1)S(1)}, bf16[1,64,5120]{2,1,0:T(8,128)(2,1)}, u32[]{:S(2)}) copy-start(bf16[1,64,5120]{2,1,0:T(8,128)(2,1)} %param.10) | copy-start | bytes 1966084
  3.2 28.3 %all-to-all-start = ((bf16[32,160,128]{2,1,0:T(8,128)(2,1)}), bf16[32,160,128]{2,1,0:T(8,128)(2,1)S(1)}, u32[]{:S(2)}, u32[]{:S(2)}) async-start(bf16[32,160,128]{2,1,0:T(8,128)(2,1)} %pack_kv.1), calls=%async_computation | async-start | bytes 2621440 | tf_op jit(solution)/shard_map/all_to_all | solution.py:290
  11.1 3.0 %copy-start.3 = (f32[5120]{0:T(1024)S(1)}, f32[5120]{0:T(1024)}, u32[]{:S(2)}) copy-start(f32[5120]{0:T(1024)} %param.14) | copy-start | bytes 61444
  11.9 2.2 %collective-permute-start.1 = (bf16[64,5248]{1,0:T(8,128)(2,1)S(1)}, bf16[64,5248]{1,0:T(8,128)(2,1)S(1)}, u32[]{:S(2)}, u32[]{:S(2)}) collective-permute-start(bf16[64,5248]{1,0:T(8,128)(2,1)S(1)} %concatenate.3), channel_id=1, source_target_pairs={{24,56},{56,88},{88,120},{120,152},{152,184},{184,216},{216,248},{... | collective-permute-start | bytes 2015240 | tf_op jit(solution)/shard_map/ppermute | solution.py:315
  12.6 23.0 %collective-permute-start = (bf16[64,5120]{1,0:T(8,128)(2,1)}, bf16[64,5120]{1,0:T(8,128)(2,1)}, u32[]{:S(2)}, u32[]{:S(2)}) collective-permute-start(bf16[64,5120]{1,0:T(8,128)(2,1)} %bitcast.3), channel_id=1, source_target_pairs={{24,56},{56,88},{88,120},{120,152},{152,184},{184,216},{216,248},{... | collective-permute-start | bytes 1966088 | tf_op jit(solution)/shard_map/ppermute | solution.py:315
  31.6 28.8 %all-to-all-start.1 = ((bf16[32,144,128]{2,1,0:T(8,128)(2,1)}), bf16[32,144,128]{2,1,0:T(8,128)(2,1)S(1)}, u32[]{:S(2)}, u32[]{:S(2)}) async-start(bf16[32,144,128]{2,1,0:T(8,128)(2,1)} %pack_q.1), calls=%async_computation.1 | async-start | bytes 2359296 | tf_op jit(solution)/shard_map/all_to_all | solution.py:290
  36.5 23.8 %copy-start.2 = (f32[128,640]{1,0:T(8,128)S(1)}, f32[128,640]{1,0:T(8,128)}, u32[]{:S(2)}) copy-start(f32[128,640]{1,0:T(8,128)} %gates.3) | copy-start | bytes 983044
  36.5 23.8 %collective-permute-start.3 = (bf16[16,160,128]{2,1,0:T(8,128)(2,1)}, bf16[16,160,128]{2,1,0:T(8,128)(2,1)S(1)}, u32[]{:S(2)}, u32[]{:S(2)}) collective-permute-start(bf16[16,160,128]{2,1,0:T(8,128)(2,1)} %slice.10), channel_id=1, source_target_pairs={{0,32},{32,64},{64,96},{96,128},{128,160},{160,192},{192,224},{224... | collective-permute-start | bytes 1966088 | tf_op jit(solution)/shard_map/ppermute | solution.py:328
  43.4 27.2 %collective-permute-start.5 = (bf16[64,5120]{1,0:T(8,128)(2,1)}, bf16[64,5120]{1,0:T(8,128)(2,1)}, u32[]{:S(2)}, u32[]{:S(2)}) collective-permute-start(bf16[64,5120]{1,0:T(8,128)(2,1)} %broadcast_select_fusion), channel_id=1, source_target_pairs={{0,8},{8,16},{16,24},{24,0},{1,9},{9,17},{17,25},{25,1},{2,10},{10... | collective-permute-start | bytes 1966088 | tf_op jit(solution)/shard_map/ppermute | solution.py:367
  48.0 11.6 %collective-permute-start.2 = (bf16[8,160,128]{2,1,0:T(8,128)(2,1)S(1)}, bf16[8,160,128]{2,1,0:T(8,128)(2,1)S(1)}, u32[]{:S(2)}, u32[]{:S(2)}) collective-permute-start(bf16[8,160,128]{2,1,0:T(8,128)(2,1)S(1)} %get-tuple-element.18), channel_id=1, source_target_pairs={{32,0},{64,32},{96,64},{128,96},{160,128},{192,160},{224,192},{256... | collective-permute-start | bytes 983048 | tf_op jit(solution)/shard_map/ppermute | solution.py:329
  49.9 17.8 %collective-permute-start.4 = (bf16[8,160,128]{2,1,0:T(8,128)(2,1)}, bf16[8,160,128]{2,1,0:T(8,128)(2,1)}, u32[]{:S(2)}, u32[]{:S(2)}) collective-permute-start(bf16[8,160,128]{2,1,0:T(8,128)(2,1)} %get-tuple-element.17), channel_id=1, source_target_pairs={{0,32},{32,64},{64,96},{96,128},{128,160},{160,192},{192,224},{224... | collective-permute-start | bytes 983048 | tf_op jit(solution)/shard_map/ppermute | solution.py:330
  59.6 0.7 copy-start.4
  60.3 1.0 copy-start.5
  70.6 26.5 %copy-start.1 = (bf16[64,5120]{1,0:T(8,128)(2,1)S(1)}, bf16[64,5120]{1,0:T(8,128)(2,1)}, u32[]{:S(2)}) copy-start(bf16[64,5120]{1,0:T(8,128)(2,1)} %incoming.1) | copy-start | bytes 1966084
